TPU v7x, 256 devices: a whole 4x4x8 slice. The times are simulated.
256 devices in a mesh: tm: 8 (over x, core), tile: 32 (over y, z).
Axes of the slice: x: 4, y: 4, z: 8, core: 2. Of those that a mesh axis runs over, the one named last changes fastest.
Arguments:
- recording: bfloat16 [262144, 1024], P('tile', 'tm'), may hold values from -300 to 300
- footprints: bfloat16 [262144, 256], P('tile'), may hold values from -0.375 to 0.375
- pattern: int32 [1024, 4], P('tile'), may hold values from 0 to 35, as said below
- decay: float32 [65536], P('tile'), may hold values from 0.96 to 1
- frame_gain: float32 [1024], P('tm'), may hold values from 0.6 to 1
- spikes: float32 [65536, 1024], P('tile', 'tm'), may hold values from 0 to 0.15
Outputs:
- spikes_out: float32 [65536, 1024], P('tile', 'tm')
- traces_last: float32 [65536, 1024], P('tile', 'tm')
Inputs may be any that keep to these rules, and one draw needn't show every extreme that they name: `pattern`: with p = q % 32, row q holds 4 different values between p and p + 4, always including p, p + 2 and p + 4, in some order; value v names the stripe's own neuron block v - 2, so values under 2 or over 2048 // 64 + 1 name edge blocks of the adjacent stripes.
All inputs are finite; a program needn't handle non-finite values.
Results may differ from a plain program's by a relative error of at most 0.00073.
Values may be sent and summed in bfloat16 or wider, within the bound.
A program may use at most 128 MiB of HBM per device.

v0:
```python
import jax
import jax.numpy as jnp
from jax import lax
from jax.sharding import PartitionSpec as P

NEU_BLOCK = 64
PIX_BLOCK = 256
K = 4
HB = 2
ITERS = 2


def entering(array, axis, combine, identity, reverse):
    length, place = (lax.axis_size(axis), lax.axis_index(axis))
    everything = jax.tree.map(lambda part: lax.all_gather(part, axis), array)
    start = jax.tree.map(
        lambda part, zero: jnp.broadcast_to(jnp.asarray(zero, part.dtype), part.shape),
        array,
        identity,
    )

    def turn(k, before):
        at = length - 1 - k if reverse else k
        reached = at > place if reverse else at < place
        new = combine(before, jax.tree.map(lambda part: part[at], everything))
        return jax.tree.map(lambda a, b: jnp.where(reached, a, b), new, before)

    return lax.fori_loop(0, length, turn, start)


def padded(array, sides, width):
    for axis, dim in sides:
        size, length = (lax.axis_size(axis), array.shape[dim])
        up = [(i, (i + 1) % size) for i in range(size - 1)]
        down = [(j, i) for i, j in up]
        last = lax.slice_in_dim(array, length - width, length, axis=dim)
        initial = lax.slice_in_dim(array, 0, width, axis=dim)
        before = lax.ppermute(last, axis, up)
        after = lax.ppermute(initial, axis, down)
        array = jnp.concatenate([before, array, after], axis=dim)
    return array


def shifted(array, axis, by):
    length = lax.axis_size(axis)
    pairs = [(i, i + by) for i in range(length) if 0 <= i + by < length]
    return lax.ppermute(array, axis, pairs)


def chain_affine(earlier, latter):
    return (earlier[0] * latter[0], latter[0] * earlier[1] + latter[1])


def tri_matmul(values, table):
    return jnp.dot(
        values, table, precision=lax.Precision.HIGHEST, preferred_element_type=jnp.float32
    )


def incoming_forward(summary):
    result = entering(
        summary, "tm", chain_affine, (jnp.ones_like(summary[0]), jnp.zeros_like(summary[1])), False
    )
    return result[1]


def incoming_backward(summary):
    result = entering(
        summary, "tm", chain_affine, (jnp.ones_like(summary[0]), jnp.zeros_like(summary[1])), True
    )
    return result[1]


def per_device(recording, footprints, pattern, decay, frame_gain, spikes):
    neurons, frames = spikes.shape
    blocks = neurons // NEU_BLOCK
    rim_rows = HB * NEU_BLOCK
    drive_gain = jnp.sqrt(1.0 - decay * decay)[:, None]
    decay_rate = decay[:, None] * frame_gain[None, :]
    back_rate = jnp.concatenate(
        [decay[:, None] * frame_gain[None, 1:], jnp.ones((neurons, 1), jnp.float32)], axis=1
    )
    foot_blocks = footprints.reshape(blocks, PIX_BLOCK, K * NEU_BLOCK)
    record = recording.astype(jnp.float32)
    row_pos = lax.broadcasted_iota(jnp.int32, (frames, frames), 0)
    col_pos = lax.broadcasted_iota(jnp.int32, (frames, frames), 1)
    upper_incl = (row_pos <= col_pos).astype(jnp.float32)
    upper_strict = (row_pos < col_pos).astype(jnp.float32)
    lower_incl = (row_pos >= col_pos).astype(jnp.float32)
    fwd_total = jnp.exp(tri_matmul(jnp.log(decay_rate), upper_incl))
    back_log = tri_matmul(jnp.log(back_rate), upper_strict)
    back_prefix = jnp.exp(back_log)
    back_total = jnp.exp(back_log[:, -1:] - back_log)
    wide_onehot = (
        pattern.reshape(1, -1) == jnp.arange(blocks + 2 * HB, dtype=jnp.int32)[:, None]
    ).astype(jnp.float32)

    def forward_pass(drive):
        local_part = fwd_total * tri_matmul(drive / fwd_total, upper_incl)
        carry_in = incoming_forward((fwd_total[:, -1], local_part[:, -1]))
        return local_part + fwd_total * carry_in[:, None]

    def footprint_apply(values):
        extended = padded(values, (("tile", 0),), rim_rows)
        picked = extended.reshape(blocks + 2 * HB, NEU_BLOCK, frames)[pattern]
        picked = picked.reshape(blocks, K * NEU_BLOCK, frames)
        fitted = jnp.einsum("paj,pjf->paf", foot_blocks, picked, preferred_element_type=jnp.float32)
        return fitted.reshape(blocks * PIX_BLOCK, frames)

    current = spikes
    traces = spikes
    for iteration in range(ITERS):
        traces = forward_pass(drive_gain * current)
        fitted = footprint_apply(traces.astype(jnp.bfloat16))
        residual = (fitted - record).astype(jnp.bfloat16)
        contrib = jnp.einsum(
            "paj,paf->pjf",
            foot_blocks,
            residual.reshape(blocks, PIX_BLOCK, frames),
            preferred_element_type=jnp.float32,
        )
        contrib = contrib.reshape(blocks * K, NEU_BLOCK * frames)
        summed = jnp.dot(
            wide_onehot,
            contrib,
            precision=lax.Precision.HIGHEST,
            preferred_element_type=jnp.float32,
        )
        summed = summed.reshape(neurons + 2 * rim_rows, frames)
        from_above = shifted(summed[:rim_rows], "tile", -1)
        from_below = shifted(summed[rim_rows + neurons :], "tile", 1)
        own_sums = summed[rim_rows : rim_rows + neurons]
        own_sums = own_sums.at[:rim_rows].add(from_below)
        backward_local_part = (
            tri_matmul(own_sums.at[neurons - rim_rows :].add(from_above) * back_prefix, lower_incl)
            / back_prefix
        )
        head = decay_rate[:, 0]
        backward_carry_in = incoming_backward(
            (head * back_total[:, 0], head * backward_local_part[:, 0])
        )
        gradient = drive_gain * (backward_local_part + back_total * backward_carry_in[:, None])
        direction = forward_pass(drive_gain * gradient).astype(jnp.bfloat16)
        projected = footprint_apply(direction)
        grad_sq, image_sq = lax.psum(
            (jnp.sum(gradient * gradient), jnp.sum(projected * projected)), ("tm", "tile")
        )
        step_size = grad_sq / (image_sq + 1e-06)
        current = jnp.maximum(current - step_size * gradient, 0.0)
    return (current, traces)


def solution(mesh):
    return jax.shard_map(
        per_device,
        mesh=mesh,
        in_specs=(
            P("tile", "tm"),
            P("tile", None),
            P("tile", None),
            P("tile"),
            P("tm"),
            P("tile", "tm"),
        ),
        out_specs=(P("tile", "tm"), P("tile", "tm")),
        check_vma=False,
    )
```

profile of v0, /device:TPU:1, one launch (start us, length us, event | category | flops | bytes accessed | tf_op | source)
XLA Modules:
  0.0 472.5 jit_solution(6232184334555677830)
XLA Ops:
  6.4 15.9 %all-gather.1 = f32[16384,1]{0,1:T(1,128)S(1)} all-gather(f32[2048,1]{0,1:T(1,128)S(1)} %slice.222), channel_id=3, replica_groups=mesh['tm'=8,'tile'=32] {'tm'}, dimensions={0}, use_global_device_ids=true | all-gather | bytes 73728 | tf_op jit(solution)/shard_map/all_gather | solution.py:15
  23.6 12.8 %all-gather = f32[16384,1]{0,1:T(1,128)S(1)} all-gather(f32[2048,1]{0,1:T(1,128)S(1)} %slice.221), channel_id=2, replica_groups=mesh['tm'=8,'tile'=32] {'tm'}, dimensions={0}, use_global_device_ids=true | all-gather | bytes 73728 | tf_op jit(solution)/shard_map/all_gather | solution.py:15
  48.6 6.3 %convolution_bitcast_fusion.3 = f32[32,256,128]{1,2,0:T(8,128)} fusion(bf16[32,256,128]{2,1,0:T(8,128)(2,1)} %bitcast.92, bf16[32,256,256]{2,1,0:T(8,128)(2,1)} %bitcast.82), kind=kOutput, calls=%fused_computation.38 | convolution fusion | flops 536870912 | bytes 10485760 | tf_op jit(solution)/shard_map/paj,pjf->paf/dot_general | solution.py:107
  54.9 5.6 %copy.21 = f32[32,256,128]{2,1,0:T(8,128)} copy(f32[32,256,128]{1,2,0:T(8,128)} %convolution_bitcast_fusion.3) | data formatting | bytes 8388608 | tf_op jit(solution)/shard_map/paj,pjf->paf/dot_general | solution.py:107
  67.4 5.6 %copy.23 = f32[32,256,128]{2,1,0:T(8,128)} copy(f32[32,256,128]{1,2,0:T(8,128)} %convolution_bitcast_fusion.2) | data formatting | bytes 8388608 | tf_op jit(solution)/shard_map/paj,paf->pjf/dot_general | solution.py:116
  73.0 5.0 %reshape.231 = f32[128,8192]{1,0:T(8,128)} reshape(f32[32,256,128]{2,1,0:T(8,128)} %copy.23) | data formatting | bytes 8388608 | tf_op jit(solution)/shard_map/reshape | solution.py:122
  84.2 4.3 collective-permute-start.2
  104.7 15.1 %all-gather.3 = f32[16384,1]{0,1:T(1,128)S(1)} all-gather(f32[2048,1]{0,1:T(1,128)S(1)} %get-tuple-element.896), channel_id=5, replica_groups=mesh['tm'=8,'tile'=32] {'tm'}, dimensions={0}, use_global_device_ids=true | all-gather | bytes 73728 | tf_op jit(solution)/shard_map/all_gather | solution.py:15
  120.6 12.8 %all-gather.2 = f32[16384,1]{0,1:T(1,128)S(1)} all-gather(f32[2048,1]{0,1:T(1,128)S(1)} %get-tuple-element.897), channel_id=4, replica_groups=mesh['tm'=8,'tile'=32] {'tm'}, dimensions={0}, use_global_device_ids=true | all-gather | bytes 73728 | tf_op jit(solution)/shard_map/all_gather | solution.py:15
  138.6 12.7 %all-gather.4 = f32[16384,1]{0,1:T(1,128)S(1)} all-gather(f32[2048,1]{0,1:T(1,128)S(1)} %slice.234), channel_id=6, replica_groups=mesh['tm'=8,'tile'=32] {'tm'}, dimensions={0}, use_global_device_ids=true | all-gather | bytes 73728 | tf_op jit(solution)/shard_map/all_gather | solution.py:15
  154.0 4.8 %collective-permute-start.4 = (bf16[128,128]{0,1:T(8,128)(2,1)S(1)}, bf16[128,128]{0,1:T(8,128)(2,1)S(1)}, u32[]{:S(2)}, u32[]{:S(2)}) collective-permute-start(bf16[128,128]{0,1:T(8,128)(2,1)S(1)} %get-tuple-element.902), channel_id=1, source_target_pairs={{0,1},{1,2},{2,3},{3,4},{4,5},{5,6},{6,7},{7,8},{8,9},{9,10},{10,1... | collective-permute-start | bytes 98312 | tf_op jit(solution)/shard_map/ppermute | solution.py:38
  166.3 5.0 %multiply_reduce_fusion.1 = f32[]{:T(128)} fusion(bf16[32,256,128]{2,1,0:T(8,128)(2,1)} %bitcast.97, bf16[32,256,256]{2,1,0:T(8,128)(2,1)} %bitcast.83), kind=kOutput, calls=%fused_computation.27 | convolution fusion | flops 538968064 | bytes 6291460 | tf_op jit(solution)/shard_map/paj,pjf->paf/dot_general | solution.py:107
  171.3 78.7 %all-reduce.2 = (f32[]{:T(128)}, f32[]{:T(128)}) all-reduce(f32[]{:T(128)} %get-tuple-element.876, f32[]{:T(128)} %multiply_reduce_fusion.1), channel_id=1, replica_groups=mesh['tm'=8,'tile'=32] {'tm','tile'}, use_global_device_ids=true, to_apply=%region_5.6 | all-reduce | flops 2 | bytes 16 | tf_op jit(solution)/shard_map/psum | solution.py:145
  254.5 13.2 %all-gather.5 = f32[16384,1]{0,1:T(1,128)S(1)} all-gather(f32[2048,1]{0,1:T(1,128)S(1)} %slice.237), channel_id=7, replica_groups=mesh['tm'=8,'tile'=32] {'tm'}, dimensions={0}, use_global_device_ids=true | all-gather | bytes 73728 | tf_op jit(solution)/shard_map/all_gather | solution.py:15
  280.7 6.3 %convolution_bitcast_fusion.1 = f32[32,256,128]{1,2,0:T(8,128)} fusion(bf16[32,256,128]{2,1,0:T(8,128)(2,1)} %bitcast.93, bf16[32,256,256]{2,1,0:T(8,128)(2,1)} %bitcast.84), kind=kOutput, calls=%fused_computation.36 | convolution fusion | flops 536870912 | bytes 10485760 | tf_op jit(solution)/shard_map/paj,pjf->paf/dot_general | solution.py:107
  287.0 5.6 %copy.33 = f32[32,256,128]{2,1,0:T(8,128)} copy(f32[32,256,128]{1,2,0:T(8,128)} %convolution_bitcast_fusion.1) | data formatting | bytes 8388608 | tf_op jit(solution)/shard_map/paj,pjf->paf/dot_general | solution.py:107
  299.5 5.6 %copy.35 = f32[32,256,128]{2,1,0:T(8,128)} copy(f32[32,256,128]{1,2,0:T(8,128)} %convolution_bitcast_fusion) | data formatting | bytes 8388608 | tf_op jit(solution)/shard_map/paj,paf->pjf/dot_general | solution.py:116
  305.1 5.0 %reshape.239 = f32[128,8192]{1,0:T(8,128)} reshape(f32[32,256,128]{2,1,0:T(8,128)} %copy.35) | data formatting | bytes 8388608 | tf_op jit(solution)/shard_map/reshape | solution.py:122
  310.1 3.8 fusion.24
  335.0 15.6 %all-gather.6 = f32[16384,1]{0,1:T(1,128)S(1)} all-gather(f32[2048,1]{0,1:T(1,128)S(1)} %slice_multiply_fusion), channel_id=8, replica_groups=mesh['tm'=8,'tile'=32] {'tm'}, dimensions={0}, use_global_device_ids=true | all-gather | bytes 73728 | tf_op jit(solution)/shard_map/all_gather | solution.py:15
  356.0 12.9 %all-gather.7 = f32[16384,1]{0,1:T(1,128)S(1)} all-gather(f32[2048,1]{0,1:T(1,128)S(1)} %slice.246), channel_id=9, replica_groups=mesh['tm'=8,'tile'=32] {'tm'}, dimensions={0}, use_global_device_ids=true | all-gather | bytes 73728 | tf_op jit(solution)/shard_map/all_gather | solution.py:15
  372.4 4.0 collective-permute-start.10
  383.9 5.1 %multiply_reduce_fusion = f32[]{:T(128)} fusion(bf16[32,256,128]{2,1,0:T(8,128)(2,1)} %bitcast.96, bf16[32,256,256]{2,1,0:T(8,128)(2,1)} %bitcast.85), kind=kOutput, calls=%fused_computation.26 | convolution fusion | flops 538968064 | bytes 6291460 | tf_op jit(solution)/shard_map/paj,pjf->paf/dot_general | solution.py:107
  389.0 78.4 %all-reduce.1 = (f32[]{:T(128)}, f32[]{:T(128)}) all-reduce(f32[]{:T(128)} %get-tuple-element.872, f32[]{:T(128)} %multiply_reduce_fusion), channel_id=1, replica_groups=mesh['tm'=8,'tile'=32] {'tm','tile'}, use_global_device_ids=true, to_apply=%region_15.16 | all-reduce | flops 2 | bytes 16 | tf_op jit(solution)/shard_map/psum | solution.py:145
  (288 shorter events, 129.5 us)
Async XLA Ops:
  6.4 36.2 %copy-start.29 = (f32[128]{0:T(128)S(1)}, f32[128]{0:T(128)}, u32[]{:S(2)}) copy-start(f32[128]{0:T(128)} %param.30) | copy-start | bytes 1540
  6.4 36.3 %copy-start.28 = (s32[32,4]{0,1:T(4,128)S(1)}, s32[32,4]{0,1:T(4,128)}, u32[]{:S(2)}) copy-start(s32[32,4]{0,1:T(4,128)} %param.28) | copy-start | bytes 1540
  6.4 36.5 %copy-start.21 = (f32[2048]{0:T(1024)S(1)}, f32[2048]{0:T(1024)}, u32[]{:S(2)}) copy-start(f32[2048]{0:T(1024)} %param.29) | copy-start | bytes 24580
  39.1 6.3 %collective-permute-start = (bf16[128,128]{0,1:T(8,128)(2,1)S(1)}, bf16[128,128]{0,1:T(8,128)(2,1)S(1)}, u32[]{:S(2)}, u32[]{:S(2)}) collective-permute-start(bf16[128,128]{0,1:T(8,128)(2,1)S(1)} %get-tuple-element.904), channel_id=1, source_target_pairs={{0,1},{1,2},{2,3},{3,4},{4,5},{5,6},{6,7},{7,8},{8,9},{9,10},{10,1... | collective-permute-start | bytes 98312 | tf_op jit(solution)/shard_map/ppermute | solution.py:38
  41.2 4.8 %collective-permute-start.1 = (bf16[128,128]{0,1:T(8,128)(2,1)S(1)}, bf16[128,128]{0,1:T(8,128)(2,1)S(1)}, u32[]{:S(2)}, u32[]{:S(2)}) collective-permute-start(bf16[128,128]{0,1:T(8,128)(2,1)S(1)} %get-tuple-element.905), channel_id=1, source_target_pairs={{1,0},{2,1},{3,2},{4,3},{5,4},{6,5},{7,6},{8,7},{9,8},{10,9},{11,1... | collective-permute-start | bytes 98312 | tf_op jit(solution)/shard_map/ppermute | solution.py:39
  84.2 11.7 %collective-permute-start.2 = (f32[128,128]{0,1:T(8,128)}, f32[128,128]{0,1:T(8,128)}, u32[]{:S(2)}, u32[]{:S(2)}) collective-permute-start(f32[128,128]{0,1:T(8,128)} %copy.24), channel_id=1, source_target_pairs={{0,1},{1,2},{2,3},{3,4},{4,5},{5,6},{6,7},{7,8},{8,9},{9,10},{10,1... | collective-permute-start | bytes 196616 | tf_op jit(solution)/shard_map/ppermute | solution.py:47
  94.4 5.8 %collective-permute-start.3 = (f32[128,128]{0,1:T(8,128)S(1)}, f32[128,128]{0,1:T(8,128)S(1)}, u32[]{:S(2)}, u32[]{:S(2)}) collective-permute-start(f32[128,128]{0,1:T(8,128)S(1)} %copy.27), channel_id=1, source_target_pairs={{1,0},{2,1},{3,2},{4,3},{5,4},{6,5},{7,6},{8,7},{9,8},{10,9},{11,1... | collective-permute-start | bytes 196616 | tf_op jit(solution)/shard_map/ppermute | solution.py:47
  101.6 32.5 %copy-start.15 = (f32[2048]{0:T(1024)S(1)}, f32[2048]{0:T(1024)}, u32[]{:S(2)}) copy-start(f32[2048]{0:T(1024)} %custom-call.1) | copy-start | bytes 24580
  101.6 33.1 %copy-start.23 = (f32[2048,1]{0,1:T(1,128)S(1)}, f32[2048,1]{0,1:T(1,128)}, u32[]{:S(2)}) copy-start(f32[2048,1]{0,1:T(1,128)} %copy-done.22) | copy-start | bytes 24580
  101.6 33.1 %copy-start.26 = (f32[2048]{0:T(1024)S(1)}, f32[2048]{0:T(1024)}, u32[]{:S(2)}) copy-start(f32[2048]{0:T(1024)} %copy-done.25) | copy-start | bytes 24580
  154.0 6.2 %collective-permute-start.4 = (bf16[128,128]{0,1:T(8,128)(2,1)S(1)}, bf16[128,128]{0,1:T(8,128)(2,1)S(1)}, u32[]{:S(2)}, u32[]{:S(2)}) collective-permute-start(bf16[128,128]{0,1:T(8,128)(2,1)S(1)} %get-tuple-element.902), channel_id=1, source_target_pairs={{0,1},{1,2},{2,3},{3,4},{4,5},{5,6},{6,7},{7,8},{8,9},{9,10},{10,1... | collective-permute-start | bytes 98312 | tf_op jit(solution)/shard_map/ppermute | solution.py:38
  158.9 4.9 %collective-permute-start.5 = (bf16[128,128]{0,1:T(8,128)(2,1)S(1)}, bf16[128,128]{0,1:T(8,128)(2,1)S(1)}, u32[]{:S(2)}, u32[]{:S(2)}) collective-permute-start(bf16[128,128]{0,1:T(8,128)(2,1)S(1)} %get-tuple-element.903), channel_id=1, source_target_pairs={{1,0},{2,1},{3,2},{4,3},{5,4},{6,5},{7,6},{8,7},{9,8},{10,9},{11,1... | collective-permute-start | bytes 98312 | tf_op jit(solution)/shard_map/ppermute | solution.py:39
  166.3 85.0 %copy-start.3 = (f32[2048,128]{0,1:T(8,128)S(1)}, f32[2048,128]{0,1:T(8,128)}, u32[]{:S(2)}) copy-start(f32[2048,128]{0,1:T(8,128)} %copy-done.2) | copy-start | bytes 3145732
  271.4 3.6 collective-permute-start.6
  273.5 4.7 collective-permute-start.7
  317.7 8.1 %collective-permute-start.8 = (f32[128,128]{0,1:T(8,128)}, f32[128,128]{0,1:T(8,128)}, u32[]{:S(2)}, u32[]{:S(2)}) collective-permute-start(f32[128,128]{0,1:T(8,128)} %copy.36), channel_id=1, source_target_pairs={{0,1},{1,2},{2,3},{3,4},{4,5},{5,6},{6,7},{7,8},{8,9},{9,10},{10,1... | collective-permute-start | bytes 196616 | tf_op jit(solution)/shard_map/ppermute | solution.py:47
  324.5 5.0 %collective-permute-start.9 = (f32[128,128]{0,1:T(8,128)S(1)}, f32[128,128]{0,1:T(8,128)S(1)}, u32[]{:S(2)}, u32[]{:S(2)}) collective-permute-start(f32[128,128]{0,1:T(8,128)S(1)} %copy.39), channel_id=1, source_target_pairs={{1,0},{2,1},{3,2},{4,3},{5,4},{6,5},{7,6},{8,7},{9,8},{10,9},{11,1... | collective-permute-start | bytes 196616 | tf_op jit(solution)/shard_map/ppermute | solution.py:47
  331.0 21.0 %copy-start.24 = (f32[2048,1]{0,1:T(1,128)S(1)}, f32[2048,1]{0,1:T(1,128)}, u32[]{:S(2)}) copy-start(f32[2048,1]{0,1:T(1,128)} %copy-done.22) | copy-start | bytes 24580
  331.0 21.0 %copy-start.27 = (f32[2048]{0:T(1024)S(1)}, f32[2048]{0:T(1024)}, u32[]{:S(2)}) copy-start(f32[2048]{0:T(1024)} %copy-done.25) | copy-start | bytes 24580
  356.0 22.0 %copy-start.7 = (f32[2048,128]{0,1:T(8,128)S(1)}, f32[2048,128]{0,1:T(8,128)}, u32[]{:S(2)}) copy-start(f32[2048,128]{0,1:T(8,128)} %get-tuple-element.875) | copy-start | bytes 3145732
  372.4 6.9 %collective-permute-start.10 = (bf16[128,128]{0,1:T(8,128)(2,1)S(1)}, bf16[128,128]{0,1:T(8,128)(2,1)S(1)}, u32[]{:S(2)}, u32[]{:S(2)}) collective-permute-start(bf16[128,128]{0,1:T(8,128)(2,1)S(1)} %get-tuple-element.898), channel_id=1, source_target_pairs={{0,1},{1,2},{2,3},{3,4},{4,5},{5,6},{6,7},{7,8},{8,9},{9,10},{10,1... | collective-permute-start | bytes 98312 | tf_op jit(solution)/shard_map/ppermute | solution.py:38
  376.4 4.9 %collective-permute-start.11 = (bf16[128,128]{0,1:T(8,128)(2,1)S(1)}, bf16[128,128]{0,1:T(8,128)(2,1)S(1)}, u32[]{:S(2)}, u32[]{:S(2)}) collective-permute-start(bf16[128,128]{0,1:T(8,128)(2,1)S(1)} %get-tuple-element.899), channel_id=1, source_target_pairs={{1,0},{2,1},{3,2},{4,3},{5,4},{6,5},{7,6},{8,7},{9,8},{10,9},{11,1... | collective-permute-start | bytes 98312 | tf_op jit(solution)/shard_map/ppermute | solution.py:39
  383.9 84.9 %copy-start.4 = (f32[2048,128]{0,1:T(8,128)S(1)}, f32[2048,128]{0,1:T(8,128)}, u32[]{:S(2)}) copy-start(f32[2048,128]{0,1:T(8,128)} %copy-done.2) | copy-start | bytes 3145732
  383.9 84.9 %copy-start.6 = (f32[2048,128]{0,1:T(8,128)S(1)}, f32[2048,128]{0,1:T(8,128)}, u32[]{:S(2)}) copy-start(f32[2048,128]{0,1:T(8,128)} %copy-done.5) | copy-start | bytes 3145732
  (18 other events, 85.3 us)
where the time goes:
time: 475 us; the launch traced here: 473 us
  blocking collectives  268 us (56%)
  local copies, waits for them, and re-layouts  72.1 us (15%)
  matrix products  47.4 us (10%)
  other arithmetic  36.1 us (8%)
  starting transfers between devices  28.4 us (6%)
  waiting for transfers between devices  14.5 us (3%)
    psum x2, blocking collectives, per_device(): lax.psum((jnp.sum(gradient * gradient), jnp.sum(projected * projected)),...  157 us
    all_gather x8, blocking collectives, entering(): everything = jax.tree.map(lambda part: lax.all_gather(part, axis), array)  111 us
    dot_general x4, matrix products, footprint_apply(): jnp.einsum('paj,pjf->paf', foot_blocks, picked, preferred_element_type=jn...  22.7 us
    unnamed x64, local copies, waits for them, and re-layouts  13.6 us
    ppermute x4, starting transfers between devices, padded(): before = lax.ppermute(last, axis, up)  13.1 us
    dot_general x8, matrix products, tri_matmul(): jnp.dot(values, table, precision=lax.Precision.HIGHEST, preferred_element...  11.4 us
    dot_general x2, local copies, waits for them, and re-layouts, footprint_apply(): jnp.einsum('paj,pjf->paf', foot_blocks, picked, preferred_element_type=jn...  11.3 us
    dot_general x2, local copies, waits for them, and re-layouts, per_device(): jnp.einsum('paj,paf->pjf', foot_blocks, residual.reshape(blocks, PIX_BLOC...  11.2 us
  transfers between devices with their start and end apart: 12, of which 6 were waited for; matrix products, arithmetic and copies ran while one was open for 4% of the time, Pallas kernels for 0%

commit v1 on v0

v1 whole, which is shorter than its diff:
```python
import functools
import itertools

import jax
import jax.numpy as jnp
from jax import lax
from jax.experimental import pallas as pl
from jax.experimental.pallas import tpu as pltpu
from jax.sharding import PartitionSpec as P

NEU_BLOCK = 64
PIX_BLOCK = 256
K = 4
HB = 2
ITERS = 2

NX, NY, NZ, NC = 4, 4, 8, 2
NT = NX * NC
NTILE = NY * NZ
FR = 128
NCOL = 18
ROWS = 24
NEU = 2048
PIX = 8192
MESH = pl.DeviceIdType.MESH
F32 = jnp.float32
BF16 = jnp.bfloat16


def ring_distance(d, n):
    return min(d, n - d)


def offsets(keep):
    found = []
    for dx, dy, dz, dc in itertools.product(range(NX), range(NY), range(NZ), range(NC)):
        if (dx, dy, dz, dc) != (0, 0, 0, 0) and keep(dx, dy, dz, dc):
            far = ring_distance(dx, NX) + ring_distance(dy, NY) + ring_distance(dz, NZ)
            found.append((-far, dx, dy, dz, dc))
    return [o[1:] for o in sorted(found)]


TM_GROUP = offsets(lambda dx, dy, dz, dc: dy == 0 and dz == 0)
PLANE_GROUP = offsets(lambda dx, dy, dz, dc: dx == 0 and dc == 0)
STAGES = (TM_GROUP, PLANE_GROUP)


def split_rows(x):
    hi = x.astype(BF16)
    lo = (x - hi.astype(F32)).astype(BF16)
    return hi, lo


def kernel(
    rec_hbm, foot_hbm, pat, decay, fgain, spk_hbm,
    out_spk, out_tr,
    foot_raw, rec_raw, spk_raw, fp, fpt, rec_t,
    cur, grad, fwd, inv, sq, xh, loc, loc2, acc_n, acc_s, val_n, val_s,
    lgb, tri_lo, tri_up, decd, tab_u, tab_e, tab_t, tab_q, tab_c, row_w, row_c,
    halo_spk, halo_dec, msg_a0, msg_a1, msg_cd, got_a0, got_a1, got_cd,
    msg_b, got_b, msg_e, got_e0, got_e1,
    ss, rs, ls,
):
    tm = lax.axis_index("tm")
    tile = lax.axis_index("tile")
    px, pc = lax.div(tm, NC), lax.rem(tm, NC)
    py, pz = lax.div(tile, NZ), lax.rem(tile, NZ)

    def device_at(o):
        dx, dy, dz, dc = o
        x = lax.rem(px + dx, NX) if dx else px
        c = lax.rem(pc + dc, NC) if dc else pc
        y = lax.rem(py + dy, NY) if dy else py
        z = lax.rem(pz + dz, NZ) if dz else pz
        return (x * NC + c, y * NZ + z)

    upper = (tm, lax.rem(tile + 1, NTILE))
    lower = (tm, lax.rem(tile + NTILE - 1, NTILE))

    load_spk = pltpu.make_async_copy(spk_hbm, spk_raw, ls.at[0])
    load_foot = pltpu.make_async_copy(foot_hbm, foot_raw, ls.at[1])
    load_rec = pltpu.make_async_copy(rec_hbm, rec_raw, ls.at[2])
    load_spk.start()
    load_foot.start()
    load_rec.start()

    group = sorted(set(TM_GROUP) | set(STAGES[0]) | set(STAGES[1]))
    barrier = pltpu.get_barrier_semaphore()
    for o in group:
        pl.semaphore_signal(barrier, inc=1, device_id=device_at(o), device_id_type=MESH)
    for d in (upper, lower):
        pl.semaphore_signal(barrier, inc=1, device_id=d, device_id_type=MESH)

    def lanes(c, width=128):
        return pl.ds(pl.multiple_of(c * width, width), width)

    row = lax.broadcasted_iota(jnp.int32, (FR, FR), 0)
    col = lax.broadcasted_iota(jnp.int32, (FR, FR), 1)
    low_half = col < NEU_BLOCK
    t_centred = (row - 63).astype(F32)

    lower_tri = (row >= col).astype(BF16)
    upper_tri = (row <= col).astype(BF16)
    tri_lo[:, :FR] = lower_tri
    tri_lo[:, FR:] = lower_tri
    tri_up[:, :FR] = upper_tri
    tri_up[:, FR:] = upper_tri

    log_fg = jnp.log(fgain[...])
    lg = jnp.sum(jnp.where(row >= col, log_fg, 0.0), axis=1, keepdims=True)
    lg_mid = lg[63:64, :]
    lg_tot = lg[127:128, :]
    lgb[...] = jnp.broadcast_to(lg - lg_mid, (FR, FR))

    msg_a0[...] = jnp.zeros_like(msg_a0)
    msg_a1[...] = jnp.zeros_like(msg_a1)
    msg_cd[...] = jnp.zeros_like(msg_cd)
    msg_a0[ROWS + NCOL : ROWS + NCOL + 1, :] = jnp.broadcast_to(lg_tot, (1, FR))
    msg_a0[ROWS + NCOL + 1 : ROWS + NCOL + 2, :] = jnp.broadcast_to(lg_mid, (1, FR))
    decd[...] = jnp.ones_like(decd)
    decd[1:17, :] = decay[...]

    def prepare(c, d, present, block):
        ld = jnp.log1p(d - 1.0)
        gain = jnp.sqrt(1.0 - d * d) * present
        lc = t_centred * ld + lgb[...]
        f = jnp.exp(lc)
        a = gain * jnp.exp(-lc)
        fwd[:, lanes(c)] = f
        inv[:, lanes(c)] = a
        hi, lo = split_rows(a * a)
        s2 = jnp.dot(tri_lo[...], jnp.concatenate([hi, lo], axis=0), preferred_element_type=F32)
        sq[:, lanes(c)] = s2
        msg_a0[pl.ds(ROWS + c, 1), :] = s2[FR - 1 : FR, :]
        s = block.T
        cur[:, lanes(c)] = s
        x = a * s
        msg_a0[pl.ds(c, 1), :] = jnp.sum(x, axis=0, keepdims=True)
        hi, lo = split_rows(x)
        xh[0:FR, lanes(c)] = hi
        xh[FR : 2 * FR, lanes(c)] = lo

    load_spk.wait()

    def own_column(k, _):
        prepare(k + 1, decd[pl.ds(k + 1, 1), :], 1.0, spk_raw[pl.ds(pl.multiple_of(k * FR, FR), FR), :])
        return 0

    lax.fori_loop(0, 16, own_column, 0)

    pl.semaphore_wait(barrier, len(group) + 2)

    def remote(src, dst, k, device):
        return pltpu.make_async_remote_copy(
            src_ref=src, dst_ref=dst, send_sem=ss.at[k], recv_sem=rs.at[k],
            device_id=device, device_id_type=MESH,
        )

    halo = [
        remote(spk_hbm.at[pl.ds(NEU - FR, FR), :], halo_spk.at[0], 0, upper),
        remote(spk_hbm.at[pl.ds(0, FR), :], halo_spk.at[1], 1, lower),
        remote(decay.at[pl.ds(8, 8), :], halo_dec.at[0], 2, upper),
        remote(decay.at[pl.ds(0, 8), :], halo_dec.at[1], 3, lower),
    ]
    for copy in halo:
        copy.start()

    def names(q, k, v):
        return jnp.where(pat[q, k] - q == v, 1.0, 0.0)

    def sources(q):
        own = [[names(q, k, v) for k in range(K)] for v in (0, 2, 4)]
        return own + [[1.0 - own[0][k] - own[1][k] - own[2][k] for k in range(K)]]

    def is_one(q):
        return sum(names(q, k, 1) for k in range(K))

    load_foot.wait()

    def arrange(q, _):
        at = pl.ds(pl.multiple_of(q * PIX_BLOCK, PIX_BLOCK), PIX_BLOCK)
        turned = foot_raw[at, :].T
        chunks = [turned[k * NEU_BLOCK : (k + 1) * NEU_BLOCK, :] for k in range(K)]
        for s, weights in enumerate(sources(q)):
            mixed = sum(chunks[k] * jnp.full((1, PIX_BLOCK), weights[k], F32).astype(BF16) for k in range(K))
            fpt[q, s * NEU_BLOCK : (s + 1) * NEU_BLOCK, :] = mixed
        fp[q] = fpt[q].T
        return 0

    lax.fori_loop(0, 32, arrange, 0)

    for copy in halo:
        copy.wait_recv()
    decd[0:1, :] = halo_dec[0, 7:8, :]
    decd[17:18, :] = halo_dec[1, 0:1, :]
    has_lower = jnp.where(tile > 0, 1.0, 0.0)
    has_upper = jnp.where(tile < NTILE - 1, 1.0, 0.0)
    prepare(0, decd[0:1, :], has_lower, halo_spk[0])
    prepare(17, decd[17:18, :], has_upper, halo_spk[1])

    def group_send(src, got, k):
        for r in range(1, NT):
            remote(src, got.at[r - 1], k, (lax.rem(tm + r, NT), tile)).start()
        got[NT - 1] = src[...]

    def group_wait(got, k):
        part = got.at[pl.ds(0, NT - 1)]
        remote(part, part, k, upper).wait_recv()

    def group_sent(got, k):
        part = got.at[pl.ds(0, NT - 1)]
        remote(part, part, k, upper).wait_send()

    def slot_of(j):
        return lax.rem(tm - j + NT - 1, NT)

    def cumulate(tri, out):
        def body(c, _):
            at = lanes(c, 256)
            out[:, at] = jnp.dot(tri[...], xh[:, at], preferred_element_type=F32)
            return 0

        lax.fori_loop(0, NCOL // 2, body, 0)

    def put_columns(value):
        def body(c, before):
            y = value(c)
            val_n[:, lanes(c)] = y.astype(BF16)
            turned = pltpu.roll(y, NEU_BLOCK, 1)
            val_s[:, lanes(c)] = jnp.where(low_half, before, turned).astype(BF16)
            return turned

        last = lax.fori_loop(0, NCOL, body, jnp.zeros((FR, FR), F32))
        val_s[:, NCOL * FR : (NCOL + 1) * FR] = last.astype(BF16)

    low_row = lax.broadcasted_iota(jnp.int32, (1, FR), 1) < NEU_BLOCK
    m_lo = jnp.where(low_row, 1.0, 0.0).astype(BF16)
    m_hi = jnp.where(low_row, 0.0, 1.0).astype(BF16)

    def pick(i):
        n0, n1, n2 = (val_n[:, lanes(i + k)] for k in range(3))
        s0, s1, s2 = (val_s[:, lanes(i + 1 + k)] for k in range(3))
        one_e, one_o = is_one(2 * i), is_one(2 * i + 1)

        def pair(x0, x1, x2, y, one):
            a = x0 * m_lo + y * m_hi
            first = jnp.where(low_row, 0.0, one).astype(BF16)
            second = jnp.where(low_row, 0.0, 1.0 - one).astype(BF16)
            b = x2 * m_lo + x0 * first + x1 * second
            return jnp.concatenate([a, b], axis=1)

        return pair(n0, n1, n2, s0, one_e), pair(s0, s1, s2, n1, one_o), one_e, one_o

    def model(i):
        even, odd, one_e, one_o = pick(i)
        y_e = jnp.dot(even, fpt[2 * i], preferred_element_type=F32)
        y_o = jnp.dot(odd, fpt[2 * i + 1], preferred_element_type=F32)
        return y_e, y_o, one_e, one_o

    def residual_step(i):
        y_e, y_o, one_e, one_o = model(i)
        r_e = (y_e - rec_t[2 * i].astype(F32)).astype(BF16)
        r_o = (y_o - rec_t[2 * i + 1].astype(F32)).astype(BF16)
        c = jnp.dot(r_e, fp[2 * i], preferred_element_type=F32)
        d = jnp.dot(r_o, fp[2 * i + 1], preferred_element_type=F32)
        ca, cb, da, db = c[:, :FR], c[:, FR:], d[:, :FR], d[:, FR:]
        acc_n[:, lanes(i)] += jnp.where(low_half, ca, cb * one_e)
        acc_s[:, lanes(i)] += jnp.where(low_half, da, ca + db * one_o)
        acc_n[:, lanes(i + 1)] += jnp.where(low_half, 0.0, cb * (1.0 - one_e) + da)
        acc_s[:, lanes(i + 1)] += jnp.where(low_half, 0.0, db * (1.0 - one_o))
        acc_n[:, lanes(i + 2)] += jnp.where(low_half, cb, 0.0)
        acc_s[:, lanes(i + 2)] += jnp.where(low_half, db, 0.0)

    def total_column(c, first=False):
        before = 0.0 if first else acc_s[:, lanes(c - 1)]
        return acc_n[:, lanes(c)] + pltpu.roll(jnp.where(low_half, acc_s[:, lanes(c)], before), NEU_BLOCK, 1)

    step = None
    for it in range(ITERS):
        msg_a, got_a, sem_a = (msg_a0, got_a0, 4) if it == 0 else (msg_a1, got_a1, 5)
        if it > 0:

            def update(c, _):
                at = lanes(c, 256)
                new = jnp.maximum(cur[:, at] - step * grad[:, at], 0.0)
                cur[:, at] = new
                x = inv[:, at] * new
                sums = jnp.sum(x, axis=0, keepdims=True)
                msg_a1[pl.ds(2 * c, 1), :] = sums[:, :FR]
                msg_a1[pl.ds(2 * c + 1, 1), :] = sums[:, FR:]
                hi, lo = split_rows(x)
                xh[0:FR, at] = hi
                xh[FR : 2 * FR, at] = lo
                return 0

            lax.fori_loop(0, NCOL // 2, update, 0)
        group_send(msg_a, got_a, sem_a)
        cumulate(tri_lo, loc)
        acc_n[...] = jnp.zeros_like(acc_n)
        acc_s[...] = jnp.zeros_like(acc_s)
        if it == 0:
            load_rec.wait()

            def turn(q, _):
                rec_t[q] = rec_raw[pl.ds(pl.multiple_of(q * PIX_BLOCK, PIX_BLOCK), PIX_BLOCK), :].T
                return 0

            lax.fori_loop(0, 32, turn, 0)
        group_wait(got_a, sem_a)
        if it == 0:
            ld = jnp.log1p(decd[...] - 1.0)
            run = None
            for j in range(NT):
                tab = got_a0.at[slot_of(j)]
                tot = tab[ROWS + NCOL : ROWS + NCOL + 1, :]
                mid = tab[ROWS + NCOL + 1 : ROWS + NCOL + 2, :]
                tab_u[j] = jnp.exp(64.0 * ld + (tot - mid))
                tab_e[j] = jnp.exp(64.0 * ld + mid)
                tab_t[j] = jnp.exp(128.0 * ld + tot)
                tab_q[j] = tab_u[j] * tab[ROWS : 2 * ROWS, :]
            run = tab_e[tm]
            for j in range(NT - 1, -1, -1):
                active = j < tm
                tab_c[j] = jnp.where(active, run * tab_u[j], 0.0)
                run = jnp.where(active, run * tab_t[j], run)
        carry = jnp.zeros((ROWS, FR), F32)
        for j in range(NT):
            carry = carry + tab_c[j] * got_a[slot_of(j), 0:ROWS, :]
        row_c[...] = carry

        def traces_of(c):
            y = fwd[:, lanes(c)] * (loc[:, lanes(c)] + row_c[pl.ds(c, 1), :])
            if it == ITERS - 1:
                loc[:, lanes(c)] = y
            return y

        put_columns(traces_of)

        def edge_blocks(k, _):
            residual_step(k + 12 * lax.div(k, 2))
            return 0

        lax.fori_loop(0, 4, edge_blocks, 0)
        msg_b[2 * it, :, :FR] = total_column(0, first=True)
        msg_b[2 * it, :, FR:] = total_column(1)
        msg_b[2 * it + 1, :, :FR] = total_column(16)
        msg_b[2 * it + 1, :, FR:] = total_column(17)
        to_low = remote(msg_b.at[2 * it], got_b.at[2 * it], 6 + 2 * it, lower)
        to_up = remote(msg_b.at[2 * it + 1], got_b.at[2 * it + 1], 7 + 2 * it, upper)
        to_low.start()
        to_up.start()

        def inner_blocks(k, _):
            residual_step(k + 2)
            return 0

        lax.fori_loop(0, 12, inner_blocks, 0)

        def back_column(c, s):
            x = fwd[:, lanes(c)] * s
            msg_cd[it, pl.ds(c, 1), :] = jnp.sum(x, axis=0, keepdims=True)
            msg_cd[it, pl.ds(ROWS + c, 1), :] = jnp.sum(x * sq[:, lanes(c)], axis=0, keepdims=True)
            hi, lo = split_rows(x)
            xh[0:FR, lanes(c)] = hi
            xh[FR : 2 * FR, lanes(c)] = lo

        def inner_column(k, _):
            back_column(k + 2, total_column(k + 2))
            return 0

        lax.fori_loop(0, 14, inner_column, 0)
        to_low.wait_recv()
        to_up.wait_recv()
        back_column(0, msg_b[2 * it, :, :FR] + has_lower * got_b[2 * it + 1, :, :FR])
        back_column(1, msg_b[2 * it, :, FR:] + has_lower * got_b[2 * it + 1, :, FR:])
        back_column(16, msg_b[2 * it + 1, :, :FR] + has_upper * got_b[2 * it, :, :FR])
        back_column(17, msg_b[2 * it + 1, :, FR:] + has_upper * got_b[2 * it, :, FR:])
        group_send(msg_cd.at[it], got_cd.at[it], 10 + it)
        cumulate(tri_up, loc2)

        def square_part(c, _):
            at = lanes(c, 256)
            a = inv[:, at]
            hi, lo = split_rows(a * a * loc2[:, at])
            both = jnp.concatenate([hi, lo], axis=0)
            grad[:, at] = jnp.dot(tri_lo[...], both, preferred_element_type=F32)
            return 0

        lax.fori_loop(0, NCOL // 2, square_part, 0)
        group_wait(got_cd.at[it], 10 + it)
        w = jnp.zeros((ROWS, FR), F32)
        mine = w
        carry = w
        for j in range(NT - 1, -1, -1):
            at = slot_of(j)
            mine = jnp.where(tm == j, w, mine)
            carry = carry + tab_c[j] * (got_cd[it, at, ROWS : 2 * ROWS, :] + tab_q[j] * w)
            w = tab_e[j] * got_cd[it, at, 0:ROWS, :] + tab_t[j] * w
        row_w[...] = tab_u[tm] * mine
        row_c[...] = carry

        def direction_of(c):
            at = lanes(c)
            return fwd[:, at] * (grad[:, at] + sq[:, at] * row_w[pl.ds(c, 1), :] + row_c[pl.ds(c, 1), :])

        put_columns(direction_of)

        def gradient_column(c):
            at = lanes(c)
            g = inv[:, at] * (loc2[:, at] + row_w[pl.ds(c, 1), :])
            grad[:, at] = g
            return g

        def image_step(i, sums):
            g_sum, p_sum = sums
            y_e, y_o, _, _ = model(i)
            p = y_e * y_e + y_o * y_o
            p_sum = p_sum + jnp.sum(p.reshape(16, 8, 256), axis=0)
            g = gradient_column(i + 1)
            g_sum = g_sum + jnp.sum((g * g).reshape(16, 8, FR), axis=0)
            return g_sum, p_sum

        g_sum, p_sum = lax.fori_loop(
            0, 16, image_step, (jnp.zeros((8, FR), F32), jnp.zeros((8, 2 * FR), F32))
        )
        g_row = jnp.sum(g_sum, axis=0, keepdims=True)
        p_row = jnp.sum(p_sum[:, :FR] + p_sum[:, FR:], axis=0, keepdims=True)
        total = jnp.where(
            low_row, g_row + pltpu.roll(g_row, NEU_BLOCK, 1), p_row + pltpu.roll(p_row, NEU_BLOCK, 1)
        )
        for k, (stage, got_e) in enumerate(zip(STAGES, (got_e0, got_e1))):
            msg_e[2 * it + k] = total
            n = len(stage)
            for i, o in enumerate(stage):
                remote(msg_e.at[2 * it + k], got_e.at[it, i], 12 + 2 * it + k, device_at(o)).start()
            if k == 0:
                if it < ITERS - 1:
                    gradient_column(0)
                    gradient_column(17)
            elif it == ITERS - 1:

                def turn_out(c, _):
                    at = lanes(c + 1)
                    to = pl.ds(pl.multiple_of(c * FR, FR), FR)
                    out_tr[to, :] = loc[:, at].T
                    spk_raw[to, :] = cur[:, at].T
                    rec32 = grad[:, at].T
                    out_spk[to, :] = rec32
                    return 0

                lax.fori_loop(0, 16, turn_out, 0)
            everything = got_e.at[it]
            remote(everything, everything, 12 + 2 * it + k, upper).wait_recv()
            parts = [total] + [got_e[it, i] for i in range(n)]
            while len(parts) > 1:
                parts = [a + b for a, b in zip(parts[::2], parts[1::2])] + parts[len(parts) // 2 * 2 :]
            total = parts[0]
        grad_sq = jnp.sum(jnp.where(low_row, total, 0.0), axis=1, keepdims=True)
        image_sq = jnp.sum(jnp.where(low_row, 0.0, total), axis=1, keepdims=True)
        step = grad_sq / (image_sq + 1e-06)

    def finish(c, _):
        to = pl.ds(pl.multiple_of(c * 256, 256), 256)
        out_spk[to, :] = jnp.maximum(spk_raw[to, :] - step * out_spk[to, :], 0.0)
        return 0

    lax.fori_loop(0, 8, finish, 0)

    for copy in halo:
        copy.wait_send()
    group_sent(got_a0, 4)
    group_sent(got_a1, 5)
    for it in range(ITERS):
        remote(msg_b.at[2 * it], got_b.at[2 * it], 6 + 2 * it, lower).wait_send()
        remote(msg_b.at[2 * it + 1], got_b.at[2 * it + 1], 7 + 2 * it, upper).wait_send()
        group_sent(got_cd.at[it], 10 + it)
        for k, got_e in enumerate((got_e0, got_e1)):
            everything = got_e.at[it]
            remote(everything, everything, 12 + 2 * it + k, upper).wait_send()


def per_device(recording, footprints, pattern, decay, frame_gain, spikes):
    wide = (FR, NCOL * FR)
    vm = pltpu.VMEM
    scratch = [
        vm((PIX, 256), BF16), vm((PIX, FR), BF16), vm((NEU, FR), F32),
        vm((32, 256, 256), BF16), vm((32, 256, 256), BF16), vm((32, FR, 256), BF16),
        vm(wide, F32), vm(wide, F32), vm(wide, F32), vm(wide, F32), vm(wide, F32),
        vm((2 * FR, NCOL * FR), BF16), vm(wide, F32), vm(wide, F32), vm(wide, F32), vm(wide, F32),
        vm(wide, BF16), vm((FR, (NCOL + 1) * FR), BF16),
        vm((FR, FR), F32), vm((FR, 2 * FR), BF16), vm((FR, 2 * FR), BF16),
        vm((ROWS, FR), F32),
        vm((NT, ROWS, FR), F32), vm((NT, ROWS, FR), F32), vm((NT, ROWS, FR), F32),
        vm((NT, ROWS, FR), F32), vm((NT, ROWS, FR), F32),
        vm((ROWS, FR), F32), vm((ROWS, FR), F32),
        vm((2, FR, FR), F32), vm((2, 8, FR), F32),
        vm((2 * ROWS, FR), F32), vm((ROWS, FR), F32), vm((ITERS, 2 * ROWS, FR), F32),
        vm((NT, 2 * ROWS, FR), F32), vm((NT, ROWS, FR), F32), vm((ITERS, NT, 2 * ROWS, FR), F32),
        vm((2 * ITERS, FR, 2 * FR), F32), vm((2 * ITERS, FR, 2 * FR), F32),
        vm((2 * ITERS, 1, FR), F32),
        vm((ITERS, len(STAGES[0]), 1, FR), F32), vm((ITERS, len(STAGES[1]), 1, FR), F32),
        pltpu.SemaphoreType.DMA((16,)), pltpu.SemaphoreType.DMA((16,)), pltpu.SemaphoreType.DMA((3,)),
    ]
    anywhere = pl.BlockSpec(memory_space=pl.ANY)
    in_vmem = pl.BlockSpec(memory_space=pltpu.VMEM)
    return pl.pallas_call(
        kernel,
        out_shape=(jax.ShapeDtypeStruct((NEU, FR), F32), jax.ShapeDtypeStruct((NEU, FR), F32)),
        in_specs=[
            anywhere, anywhere, pl.BlockSpec(memory_space=pltpu.SMEM), in_vmem, in_vmem, anywhere,
        ],
        out_specs=(in_vmem, in_vmem),
        scratch_shapes=scratch,
        compiler_params=pltpu.CompilerParams(
            collective_id=0, has_side_effects=True, vmem_limit_bytes=60 * 2**20
        ),
        name="deconvolve",
    )(
        recording, footprints, pattern, decay.reshape(16, FR), frame_gain.reshape(1, FR), spikes,
    )


def solution(mesh):
    return jax.shard_map(
        per_device,
        mesh=mesh,
        in_specs=(
            P("tile", "tm"),
            P("tile", None),
            P("tile", None),
            P("tile"),
            P("tm"),
            P("tile", "tm"),
        ),
        out_specs=(P("tile", "tm"), P("tile", "tm")),
        check_vma=False,
    )
```

time: 475 us -> 89.9 us (0.19)
  blocking collectives: 268 us -> 0 us
  Pallas kernels: 0 us -> 83.2 us
  local copies, waits for them, and re-layouts: 72.1 us -> 5.89 us
  matrix products: 47.4 us -> 0 us
  other arithmetic: 36.1 us -> 0 us
  starting transfers between devices: 28.4 us -> 0 us
  waiting for transfers between devices: 14.5 us -> 0 us
    psum x2 -> x0, blocking collectives: 157 us -> none  [per_device(): lax.psum((jnp.sum(gradient * gradient), jnp.sum(projected * projected)),...]
    all_gather x8 -> x0, blocking collectives: 111 us -> none  [entering(): everything = jax.tree.map(lambda part: lax.all_gather(part, axis), array)]
    pallas_call x0 -> x1, Pallas kernels: none -> 83.2 us  [per_device(): pl.pallas_call(kernel, out_shape=(jax.ShapeDtypeStruct((NEU, FR), F32), j...]
    dot_general x16 -> x0, matrix products: 47.4 us -> none  [the longest x4 22.7 us: footprint_apply(): jnp.einsum('paj,pjf->paf', foot_blocks, picked, preferred_element_type=jn...]
    ppermute x12 -> x0, starting transfers between devices: 28.4 us -> none  [the longest x4 13.1 us: padded(): before = lax.ppermute(last, axis, up)]
    dot_general x4 -> x0, local copies, waits for them, and re-layouts: 22.4 us -> none  [the longest x2 11.3 us: footprint_apply(): jnp.einsum('paj,pjf->paf', foot_blocks, picked, preferred_element_type=jn...]
    ppermute x12 -> x0, waiting for transfers between devices: 14.5 us -> none  [the longest x4 9.46 us: padded(): after = lax.ppermute(initial, axis, down)]
    slice x27 -> x0, local copies, waits for them, and re-layouts: 14.2 us -> none  [the longest x6 7.59 us: per_device(): own_sums = summed[rim_rows:rim_rows + neurons]]
  transfers between devices with their start and end apart: 12 -> 0, of which waited for: 6 -> 0; matrix products, arithmetic and copies ran while one was open for 4% -> 0% of each run, Pallas kernels for 0% -> 0%
where the time goes in v1:
time: 89.9 us; the launch traced here: 89.7 us
  Pallas kernels  83.2 us (93%)
  local copies, waits for them, and re-layouts  5.89 us (7%)
    pallas_call x1, Pallas kernels, per_device(): pl.pallas_call(kernel, out_shape=(jax.ShapeDtypeStruct((NEU, FR), F32), j...  83.2 us
    unnamed x3, local copies, waits for them, and re-layouts  5.89 us

profile of v1, /device:TPU:1, one launch (start us, length us, event | category | flops | bytes accessed | tf_op | source)
XLA Modules:
  0.0 89.7 jit_solution(5745032080355566573)
XLA Ops:
  0.6 1.4 %copy.8.pat = s32[32,4]{1,0:T(8,128)} copy(s32[32,4]{0,1:T(4,128)} %param.8) | data formatting | bytes 1024 | tf_op args[2]
  2.0 83.2 %deconvolve.1 = (f32[2048,128]{1,0:T(8,128)}, f32[2048,128]{1,0:T(8,128)}) custom-call(bf16[8192,128]{1,0:T(8,128)(2,1)} %rec_hbm.1, bf16[8192,256]{1,0:T(8,128)(2,1)} %foot_hbm.1, s32[32,4]{1,0:T(8,128)} %copy.8.pat, f32[16,128]{1,0:T(8,128)} %bitcast.2, f32[1,128]{1,0:T(1,128)} %bitcast.3, f32[2048,128]{1,0:T(8,128)} %spk_hbm.1), custom_call_target="tpu_custom_call" | custom-call | tf_op jit(solution)/shard_map/deconvolve/pallas_call | solution.py:506
  85.2 2.3 %copy.11 = f32[2048,128]{1,0:T(8,128)} copy(f32[2048,128]{1,0:T(8,128)} %get-tuple-element.4) | data formatting | bytes 2097152
  87.4 2.3 %copy.12 = f32[2048,128]{1,0:T(8,128)} copy(f32[2048,128]{1,0:T(8,128)} %get-tuple-element.5) | data formatting | bytes 2097152

commit v2 on v1

--- a/solution.py
+++ b/solution.py
@@ -41,8 +41,9 @@
 
 
 TM_GROUP = offsets(lambda dx, dy, dz, dc: dy == 0 and dz == 0)
-PLANE_GROUP = offsets(lambda dx, dy, dz, dc: dx == 0 and dc == 0)
-STAGES = (TM_GROUP, PLANE_GROUP)
+CORE_GROUP = offsets(lambda dx, dy, dz, dc: dx == 0 and dy == 0 and dz == 0)
+CHIP_GROUP = offsets(lambda dx, dy, dz, dc: dc == 0)
+STAGES = (CORE_GROUP, CHIP_GROUP)
 
 
 def split_rows(x):
@@ -52,9 +53,9 @@
 
 
 def kernel(
-    rec_hbm, foot_hbm, pat, decay, fgain, spk_hbm,
+    rec_hbm, foot_hbm, pat_hbm, dec_hbm, gain_hbm, spk_hbm,
     out_spk, out_tr,
-    foot_raw, rec_raw, spk_raw, fp, fpt, rec_t,
+    foot_raw, rec_raw, spk_raw, decay, fgain, pat, fp, fpt, rec_t,
     cur, grad, fwd, inv, sq, xh, loc, loc2, acc_n, acc_s, val_n, val_s,
     lgb, tri_lo, tri_up, decd, tab_u, tab_e, tab_t, tab_q, tab_c, row_w, row_c,
     halo_spk, halo_dec, msg_a0, msg_a1, msg_cd, got_a0, got_a1, got_cd,
@@ -77,19 +78,21 @@
     upper = (tm, lax.rem(tile + 1, NTILE))
     lower = (tm, lax.rem(tile + NTILE - 1, NTILE))
 
-    load_spk = pltpu.make_async_copy(spk_hbm, spk_raw, ls.at[0])
-    load_foot = pltpu.make_async_copy(foot_hbm, foot_raw, ls.at[1])
-    load_rec = pltpu.make_async_copy(rec_hbm, rec_raw, ls.at[2])
-    load_spk.start()
-    load_foot.start()
-    load_rec.start()
-
-    group = sorted(set(TM_GROUP) | set(STAGES[0]) | set(STAGES[1]))
+    group = offsets(lambda *o: o in TM_GROUP or o in CORE_GROUP or o in CHIP_GROUP)
     barrier = pltpu.get_barrier_semaphore()
     for o in group:
         pl.semaphore_signal(barrier, inc=1, device_id=device_at(o), device_id_type=MESH)
     for d in (upper, lower):
         pl.semaphore_signal(barrier, inc=1, device_id=d, device_id_type=MESH)
+
+    load_dec = pltpu.make_async_copy(dec_hbm, decay, ls.at[3])
+    load_gain = pltpu.make_async_copy(gain_hbm, fgain, ls.at[4])
+    load_pat = pltpu.make_async_copy(pat_hbm, pat, ls.at[5])
+    load_spk = pltpu.make_async_copy(spk_hbm, spk_raw, ls.at[0])
+    load_foot = pltpu.make_async_copy(foot_hbm, foot_raw, ls.at[1])
+    load_rec = pltpu.make_async_copy(rec_hbm, rec_raw, ls.at[2])
+    for load in (load_dec, load_gain, load_pat, load_spk, load_foot, load_rec):
+        load.start()
 
     def lanes(c, width=128):
         return pl.ds(pl.multiple_of(c * width, width), width)
@@ -106,6 +109,7 @@
     tri_up[:, :FR] = upper_tri
     tri_up[:, FR:] = upper_tri
 
+    load_gain.wait()
     log_fg = jnp.log(fgain[...])
     lg = jnp.sum(jnp.where(row >= col, log_fg, 0.0), axis=1, keepdims=True)
     lg_mid = lg[63:64, :]
@@ -118,6 +122,7 @@
     msg_a0[ROWS + NCOL : ROWS + NCOL + 1, :] = jnp.broadcast_to(lg_tot, (1, FR))
     msg_a0[ROWS + NCOL + 1 : ROWS + NCOL + 2, :] = jnp.broadcast_to(lg_mid, (1, FR))
     decd[...] = jnp.ones_like(decd)
+    load_dec.wait()
     decd[1:17, :] = decay[...]
 
     def prepare(c, d, present, block):
@@ -146,27 +151,10 @@
         prepare(k + 1, decd[pl.ds(k + 1, 1), :], 1.0, spk_raw[pl.ds(pl.multiple_of(k * FR, FR), FR), :])
         return 0
 
-    lax.fori_loop(0, 16, own_column, 0)
-
-    pl.semaphore_wait(barrier, len(group) + 2)
-
-    def remote(src, dst, k, device):
-        return pltpu.make_async_remote_copy(
-            src_ref=src, dst_ref=dst, send_sem=ss.at[k], recv_sem=rs.at[k],
-            device_id=device, device_id_type=MESH,
-        )
-
-    halo = [
-        remote(spk_hbm.at[pl.ds(NEU - FR, FR), :], halo_spk.at[0], 0, upper),
-        remote(spk_hbm.at[pl.ds(0, FR), :], halo_spk.at[1], 1, lower),
-        remote(decay.at[pl.ds(8, 8), :], halo_dec.at[0], 2, upper),
-        remote(decay.at[pl.ds(0, 8), :], halo_dec.at[1], 3, lower),
-    ]
-    for copy in halo:
-        copy.start()
+    lax.fori_loop(0, 16, own_column, 0, unroll=4)
 
     def names(q, k, v):
-        return jnp.where(pat[q, k] - q == v, 1.0, 0.0)
+        return jnp.where(pat[k, q] - q == v, 1.0, 0.0)
 
     def sources(q):
         own = [[names(q, k, v) for k in range(K)] for v in (0, 2, 4)]
@@ -175,6 +163,7 @@
     def is_one(q):
         return sum(names(q, k, 1) for k in range(K))
 
+    load_pat.wait()
     load_foot.wait()
 
     def arrange(q, _):
@@ -187,7 +176,27 @@
         fp[q] = fpt[q].T
         return 0
 
-    lax.fori_loop(0, 32, arrange, 0)
+
+    lax.fori_loop(0, 16, arrange, 0, unroll=4)
+
+    pl.semaphore_wait(barrier, len(group) + 2)
+
+    def remote(src, dst, k, device):
+        return pltpu.make_async_remote_copy(
+            src_ref=src, dst_ref=dst, send_sem=ss.at[k], recv_sem=rs.at[k],
+            device_id=device, device_id_type=MESH,
+        )
+
+    halo = [
+        remote(spk_hbm.at[pl.ds(NEU - FR, FR), :], halo_spk.at[0], 0, upper),
+        remote(spk_hbm.at[pl.ds(0, FR), :], halo_spk.at[1], 1, lower),
+        remote(decay.at[pl.ds(8, 8), :], halo_dec.at[0], 2, upper),
+        remote(decay.at[pl.ds(0, 8), :], halo_dec.at[1], 3, lower),
+    ]
+    for copy in halo:
+        copy.start()
+
+    lax.fori_loop(16, 32, arrange, 0, unroll=4)
 
     for copy in halo:
         copy.wait_recv()
@@ -220,7 +229,7 @@
             out[:, at] = jnp.dot(tri[...], xh[:, at], preferred_element_type=F32)
             return 0
 
-        lax.fori_loop(0, NCOL // 2, body, 0)
+        lax.fori_loop(0, NCOL // 2, body, 0, unroll=9)
 
     def put_columns(value):
         def body(c, before):
@@ -230,7 +239,7 @@
             val_s[:, lanes(c)] = jnp.where(low_half, before, turned).astype(BF16)
             return turned
 
-        last = lax.fori_loop(0, NCOL, body, jnp.zeros((FR, FR), F32))
+        last = lax.fori_loop(0, NCOL, body, jnp.zeros((FR, FR), F32), unroll=6)
         val_s[:, NCOL * FR : (NCOL + 1) * FR] = last.astype(BF16)
 
     low_row = lax.broadcasted_iota(jnp.int32, (1, FR), 1) < NEU_BLOCK
@@ -293,7 +302,7 @@
                 xh[FR : 2 * FR, at] = lo
                 return 0
 
-            lax.fori_loop(0, NCOL // 2, update, 0)
+            lax.fori_loop(0, NCOL // 2, update, 0, unroll=3)
         group_send(msg_a, got_a, sem_a)
         cumulate(tri_lo, loc)
         acc_n[...] = jnp.zeros_like(acc_n)
@@ -305,7 +314,7 @@
                 rec_t[q] = rec_raw[pl.ds(pl.multiple_of(q * PIX_BLOCK, PIX_BLOCK), PIX_BLOCK), :].T
                 return 0
 
-            lax.fori_loop(0, 32, turn, 0)
+            lax.fori_loop(0, 32, turn, 0, unroll=8)
         group_wait(got_a, sem_a)
         if it == 0:
             ld = jnp.log1p(decd[...] - 1.0)
@@ -340,7 +349,7 @@
             residual_step(k + 12 * lax.div(k, 2))
             return 0
 
-        lax.fori_loop(0, 4, edge_blocks, 0)
+        lax.fori_loop(0, 4, edge_blocks, 0, unroll=4)
         msg_b[2 * it, :, :FR] = total_column(0, first=True)
         msg_b[2 * it, :, FR:] = total_column(1)
         msg_b[2 * it + 1, :, :FR] = total_column(16)
@@ -354,7 +363,7 @@
             residual_step(k + 2)
             return 0
 
-        lax.fori_loop(0, 12, inner_blocks, 0)
+        lax.fori_loop(0, 12, inner_blocks, 0, unroll=12)
 
         def back_column(c, s):
             x = fwd[:, lanes(c)] * s
@@ -368,7 +377,7 @@
             back_column(k + 2, total_column(k + 2))
             return 0
 
-        lax.fori_loop(0, 14, inner_column, 0)
+        lax.fori_loop(0, 14, inner_column, 0, unroll=7)
         to_low.wait_recv()
         to_up.wait_recv()
         back_column(0, msg_b[2 * it, :, :FR] + has_lower * got_b[2 * it + 1, :, :FR])
@@ -386,7 +395,7 @@
             grad[:, at] = jnp.dot(tri_lo[...], both, preferred_element_type=F32)
             return 0
 
-        lax.fori_loop(0, NCOL // 2, square_part, 0)
+        lax.fori_loop(0, NCOL // 2, square_part, 0, unroll=9)
         group_wait(got_cd.at[it], 10 + it)
         w = jnp.zeros((ROWS, FR), F32)
         mine = w
@@ -421,7 +430,7 @@
             return g_sum, p_sum
 
         g_sum, p_sum = lax.fori_loop(
-            0, 16, image_step, (jnp.zeros((8, FR), F32), jnp.zeros((8, 2 * FR), F32))
+            0, 16, image_step, (jnp.zeros((8, FR), F32), jnp.zeros((8, 2 * FR), F32)), unroll=16
         )
         g_row = jnp.sum(g_sum, axis=0, keepdims=True)
         p_row = jnp.sum(p_sum[:, :FR] + p_sum[:, FR:], axis=0, keepdims=True)
@@ -448,7 +457,7 @@
                     out_spk[to, :] = rec32
                     return 0
 
-                lax.fori_loop(0, 16, turn_out, 0)
+                lax.fori_loop(0, 16, turn_out, 0, unroll=4)
             everything = got_e.at[it]
             remote(everything, everything, 12 + 2 * it + k, upper).wait_recv()
             parts = [total] + [got_e[it, i] for i in range(n)]
@@ -464,7 +473,7 @@
         out_spk[to, :] = jnp.maximum(spk_raw[to, :] - step * out_spk[to, :], 0.0)
         return 0
 
-    lax.fori_loop(0, 8, finish, 0)
+    lax.fori_loop(0, 8, finish, 0, unroll=4)
 
     for copy in halo:
         copy.wait_send()
@@ -484,6 +493,7 @@
     vm = pltpu.VMEM
     scratch = [
         vm((PIX, 256), BF16), vm((PIX, FR), BF16), vm((NEU, FR), F32),
+        vm((16, FR), F32), vm((1, FR), F32), pltpu.SMEM((K, 32), jnp.int32),
         vm((32, 256, 256), BF16), vm((32, 256, 256), BF16), vm((32, FR, 256), BF16),
         vm(wide, F32), vm(wide, F32), vm(wide, F32), vm(wide, F32), vm(wide, F32),
         vm((2 * FR, NCOL * FR), BF16), vm(wide, F32), vm(wide, F32), vm(wide, F32), vm(wide, F32),
@@ -499,15 +509,15 @@
         vm((2 * ITERS, FR, 2 * FR), F32), vm((2 * ITERS, FR, 2 * FR), F32),
         vm((2 * ITERS, 1, FR), F32),
         vm((ITERS, len(STAGES[0]), 1, FR), F32), vm((ITERS, len(STAGES[1]), 1, FR), F32),
-        pltpu.SemaphoreType.DMA((16,)), pltpu.SemaphoreType.DMA((16,)), pltpu.SemaphoreType.DMA((3,)),
+        pltpu.SemaphoreType.DMA((16,)), pltpu.SemaphoreType.DMA((16,)), pltpu.SemaphoreType.DMA((6,)),
     ]
     anywhere = pl.BlockSpec(memory_space=pl.ANY)
     in_vmem = pl.BlockSpec(memory_space=pltpu.VMEM)
     return pl.pallas_call(
         kernel,
-        out_shape=(jax.ShapeDtypeStruct((NEU, FR), F32), jax.ShapeDtypeStruct((NEU, FR), F32)),
+        out_shape=(pltpu.VMEM((NEU, FR), F32), pltpu.VMEM((NEU, FR), F32)),
         in_specs=[
-            anywhere, anywhere, pl.BlockSpec(memory_space=pltpu.SMEM), in_vmem, in_vmem, anywhere,
+            anywhere, anywhere, anywhere, anywhere, anywhere, anywhere,
         ],
         out_specs=(in_vmem, in_vmem),
         scratch_shapes=scratch,
@@ -516,7 +526,7 @@
         ),
         name="deconvolve",
     )(
-        recording, footprints, pattern, decay.reshape(16, FR), frame_gain.reshape(1, FR), spikes,
+        recording, footprints, pattern.T, decay.reshape(16, FR), frame_gain.reshape(1, FR), spikes,
     )
 
 

time: 89.9 us -> 71.4 us (0.79)
  Pallas kernels: 83.2 us -> 68.7 us
  local copies, waits for them, and re-layouts: 5.89 us -> 1.94 us
    pallas_call x1, Pallas kernels: 83.2 us -> 68.7 us  [per_device(): pl.pallas_call(kernel, out_shape=(pltpu.VMEM((NEU, FR), F32), pltpu.VMEM(...]
    unnamed x3 -> x2, local copies, waits for them, and re-layouts: 5.89 us -> 1.94 us
where the time goes in v2:
time: 71.4 us; the launch traced here: 71.3 us
  Pallas kernels  68.7 us (96%)
  local copies, waits for them, and re-layouts  1.94 us (3%)
    pallas_call x1, Pallas kernels, per_device(): pl.pallas_call(kernel, out_shape=(pltpu.VMEM((NEU, FR), F32), pltpu.VMEM(...  68.7 us
    unnamed x2, local copies, waits for them, and re-layouts  1.94 us

profile of v2, /device:TPU:1, one launch (start us, length us, event | category | flops | bytes accessed | tf_op | source)
XLA Modules:
  0.0 71.3 jit_solution(17980626341497209585)
XLA Ops:
  0.6 68.7 %deconvolve.1 = (f32[2048,128]{1,0:T(8,128)S(1)}, f32[2048,128]{1,0:T(8,128)S(1)}) custom-call(bf16[8192,128]{1,0:T(8,128)(2,1)} %rec_hbm.1, bf16[8192,256]{1,0:T(8,128)(2,1)} %foot_hbm.1, s32[4,32]{1,0:T(4,128)} %bitcast.4, f32[16,128]{1,0:T(8,128)} %bitcast.3, f32[1,128]{1,0:T(1,128)} %bitcast.5, f32[2048,128]{1,0:T(8,128)} %spk_hbm.1), custom_call_target="tpu_custom_call" | custom-call | tf_op jit(solution)/shard_map/deconvolve/pallas_call | solution.py:516
  69.3 1.0 %copy.10 = f32[2048,128]{1,0:T(8,128)} copy(f32[2048,128]{1,0:T(8,128)S(1)} %get-tuple-element.2) | data formatting | bytes 2097152
  70.3 1.0 %copy.11 = f32[2048,128]{1,0:T(8,128)} copy(f32[2048,128]{1,0:T(8,128)S(1)} %get-tuple-element.3) | data formatting | bytes 2097152

commit v3 on v2

--- a/solution.py
+++ b/solution.py
@@ -59,7 +59,7 @@
     cur, grad, fwd, inv, sq, xh, loc, loc2, acc_n, acc_s, val_n, val_s,
     lgb, tri_lo, tri_up, decd, tab_u, tab_e, tab_t, tab_q, tab_c, row_w, row_c,
     halo_spk, halo_dec, msg_a0, msg_a1, msg_cd, got_a0, got_a1, got_cd,
-    msg_b, got_b, msg_e, got_e0, got_e1,
+    msg_b, got_b, msg_h, got_h, msg_e, got_e0, got_e1,
     ss, rs, ls,
 ):
     tm = lax.axis_index("tm")
@@ -79,10 +79,12 @@
     lower = (tm, lax.rem(tile + NTILE - 1, NTILE))
 
     group = offsets(lambda *o: o in TM_GROUP or o in CORE_GROUP or o in CHIP_GROUP)
+    sides = ((0, 1), (1, NTILE - 1))
+    crossed = [(lax.rem(tm + k, NT), lax.rem(tile + by, NTILE)) for _, by in sides for k in range(1, NT, 2)]
     barrier = pltpu.get_barrier_semaphore()
     for o in group:
         pl.semaphore_signal(barrier, inc=1, device_id=device_at(o), device_id_type=MESH)
-    for d in (upper, lower):
+    for d in crossed:
         pl.semaphore_signal(barrier, inc=1, device_id=d, device_id_type=MESH)
 
     load_dec = pltpu.make_async_copy(dec_hbm, decay, ls.at[3])
@@ -125,7 +127,7 @@
     load_dec.wait()
     decd[1:17, :] = decay[...]
 
-    def prepare(c, d, present, block):
+    def prepare(c, d, present, block, own):
         ld = jnp.log1p(d - 1.0)
         gain = jnp.sqrt(1.0 - d * d) * present
         lc = t_centred * ld + lgb[...]
@@ -136,11 +138,13 @@
         hi, lo = split_rows(a * a)
         s2 = jnp.dot(tri_lo[...], jnp.concatenate([hi, lo], axis=0), preferred_element_type=F32)
         sq[:, lanes(c)] = s2
-        msg_a0[pl.ds(ROWS + c, 1), :] = s2[FR - 1 : FR, :]
+        if own:
+            msg_a0[pl.ds(ROWS + c, 1), :] = s2[FR - 1 : FR, :]
         s = block.T
         cur[:, lanes(c)] = s
         x = a * s
-        msg_a0[pl.ds(c, 1), :] = jnp.sum(x, axis=0, keepdims=True)
+        if own:
+            msg_a0[pl.ds(c, 1), :] = jnp.sum(x, axis=0, keepdims=True)
         hi, lo = split_rows(x)
         xh[0:FR, lanes(c)] = hi
         xh[FR : 2 * FR, lanes(c)] = lo
@@ -148,7 +152,7 @@
     load_spk.wait()
 
     def own_column(k, _):
-        prepare(k + 1, decd[pl.ds(k + 1, 1), :], 1.0, spk_raw[pl.ds(pl.multiple_of(k * FR, FR), FR), :])
+        prepare(k + 1, decd[pl.ds(k + 1, 1), :], 1.0, spk_raw[pl.ds(pl.multiple_of(k * FR, FR), FR), :], True)
         return 0
 
     lax.fori_loop(0, 16, own_column, 0, unroll=4)
@@ -179,7 +183,7 @@
 
     lax.fori_loop(0, 16, arrange, 0, unroll=4)
 
-    pl.semaphore_wait(barrier, len(group) + 2)
+    pl.semaphore_wait(barrier, len(group) + len(crossed))
 
     def remote(src, dst, k, device):
         return pltpu.make_async_remote_copy(
@@ -187,6 +191,43 @@
             device_id=device, device_id_type=MESH,
         )
 
+    def group_send(src, got, k):
+        for r in range(1, NT):
+            remote(src, got.at[r - 1], k, (lax.rem(tm + r, NT), tile)).start()
+        got[NT - 1] = src[...]
+
+    def group_wait(got, k):
+        part = got.at[pl.ds(0, NT - 1)]
+        remote(part, part, k, upper).wait_recv()
+
+    def group_sent(got, k):
+        part = got.at[pl.ds(0, NT - 1)]
+        remote(part, part, k, upper).wait_send()
+
+    def slot_of(j):
+        return lax.rem(tm - j + NT - 1, NT)
+
+    def wide_send(src, got, k):
+        for side, by in sides:
+            for r in range(NT):
+                to = (lax.rem(tm + r, NT), lax.rem(tile + by, NTILE))
+                remote(src.at[side], got.at[side, (r + NT - 1) % NT], k + side, to).start()
+
+    def wide_wait(got, k):
+        for side, _ in sides:
+            remote(got.at[side], got.at[side], k + side, upper).wait_recv()
+
+    def wide_sent(got, k):
+        for side, _ in sides:
+            remote(got.at[side], got.at[side], k + side, upper).wait_send()
+
+    msg_h[0] = jnp.zeros_like(msg_h[0])
+    msg_h[0, 0, 0:1, :] = msg_a0[16:17, :]
+    msg_h[0, 0, 1:2, :] = msg_a0[ROWS + 16 : ROWS + 17, :]
+    msg_h[0, 1, 0:1, :] = msg_a0[1:2, :]
+    msg_h[0, 1, 1:2, :] = msg_a0[ROWS + 1 : ROWS + 2, :]
+    wide_send(msg_h.at[0], got_h.at[0], 16)
+    group_send(msg_a0, got_a0, 4)
     halo = [
         remote(spk_hbm.at[pl.ds(NEU - FR, FR), :], halo_spk.at[0], 0, upper),
         remote(spk_hbm.at[pl.ds(0, FR), :], halo_spk.at[1], 1, lower),
@@ -198,38 +239,30 @@
 
     lax.fori_loop(16, 32, arrange, 0, unroll=4)
 
+    load_rec.wait()
+
+    def turn(q, _):
+        rec_t[q] = rec_raw[pl.ds(pl.multiple_of(q * PIX_BLOCK, PIX_BLOCK), PIX_BLOCK), :].T
+        return 0
+
+    lax.fori_loop(0, 32, turn, 0, unroll=8)
+
     for copy in halo:
         copy.wait_recv()
     decd[0:1, :] = halo_dec[0, 7:8, :]
     decd[17:18, :] = halo_dec[1, 0:1, :]
     has_lower = jnp.where(tile > 0, 1.0, 0.0)
     has_upper = jnp.where(tile < NTILE - 1, 1.0, 0.0)
-    prepare(0, decd[0:1, :], has_lower, halo_spk[0])
-    prepare(17, decd[17:18, :], has_upper, halo_spk[1])
-
-    def group_send(src, got, k):
-        for r in range(1, NT):
-            remote(src, got.at[r - 1], k, (lax.rem(tm + r, NT), tile)).start()
-        got[NT - 1] = src[...]
-
-    def group_wait(got, k):
-        part = got.at[pl.ds(0, NT - 1)]
-        remote(part, part, k, upper).wait_recv()
-
-    def group_sent(got, k):
-        part = got.at[pl.ds(0, NT - 1)]
-        remote(part, part, k, upper).wait_send()
-
-    def slot_of(j):
-        return lax.rem(tm - j + NT - 1, NT)
-
-    def cumulate(tri, out):
+    prepare(0, decd[0:1, :], has_lower, halo_spk[0], False)
+    prepare(17, decd[17:18, :], has_upper, halo_spk[1], False)
+
+    def cumulate(tri, out, first=0, last=NCOL // 2):
         def body(c, _):
             at = lanes(c, 256)
             out[:, at] = jnp.dot(tri[...], xh[:, at], preferred_element_type=F32)
             return 0
 
-        lax.fori_loop(0, NCOL // 2, body, 0, unroll=9)
+        lax.fori_loop(first, last, body, 0, unroll=last - first)
 
     def put_columns(value):
         def body(c, before):
@@ -303,20 +336,17 @@
                 return 0
 
             lax.fori_loop(0, NCOL // 2, update, 0, unroll=3)
-        group_send(msg_a, got_a, sem_a)
+            group_send(msg_a, got_a, sem_a)
         cumulate(tri_lo, loc)
         acc_n[...] = jnp.zeros_like(acc_n)
         acc_s[...] = jnp.zeros_like(acc_s)
-        if it == 0:
-            load_rec.wait()
-
-            def turn(q, _):
-                rec_t[q] = rec_raw[pl.ds(pl.multiple_of(q * PIX_BLOCK, PIX_BLOCK), PIX_BLOCK), :].T
-                return 0
-
-            lax.fori_loop(0, 32, turn, 0, unroll=8)
         group_wait(got_a, sem_a)
         if it == 0:
+            wide_wait(got_h.at[0], 16)
+            for k in range(NT):
+                for part, at in ((0, 0), (1, ROWS)):
+                    got_a0[k, at : at + 1, :] = has_lower * got_h[0, 0, k, part : part + 1, :]
+                    got_a0[k, at + 17 : at + 18, :] = has_upper * got_h[0, 1, k, part : part + 1, :]
             ld = jnp.log1p(decd[...] - 1.0)
             run = None
             for j in range(NT):
@@ -359,33 +389,47 @@
         to_low.start()
         to_up.start()
 
+        def sum_column(c, x):
+            msg_cd[it, pl.ds(c, 1), :] = jnp.sum(x, axis=0, keepdims=True)
+            msg_cd[it, pl.ds(ROWS + c, 1), :] = jnp.sum(x * sq[:, lanes(c)], axis=0, keepdims=True)
+
+        def split_column(c, x):
+            hi, lo = split_rows(x)
+            xh[0:FR, lanes(c)] = hi
+            xh[FR : 2 * FR, lanes(c)] = lo
+
+        for c, part, half in ((0, 2 * it, 0), (1, 2 * it, 1), (16, 2 * it + 1, 0), (17, 2 * it + 1, 1)):
+            sum_column(c, fwd[:, lanes(c)] * msg_b[part, :, half * FR : (half + 1) * FR])
+        msg_h[1 + it] = jnp.zeros_like(msg_h[1 + it])
+        for side, c in ((0, 16), (1, 0)):
+            msg_h[1 + it, side, 0:2, :] = msg_cd[it, c : c + 2, :]
+            msg_h[1 + it, side, 2:4, :] = msg_cd[it, ROWS + c : ROWS + c + 2, :]
+        wide_send(msg_h.at[1 + it], got_h.at[1 + it], 18 + 2 * it)
+
         def inner_blocks(k, _):
             residual_step(k + 2)
             return 0
 
         lax.fori_loop(0, 12, inner_blocks, 0, unroll=12)
 
-        def back_column(c, s):
-            x = fwd[:, lanes(c)] * s
-            msg_cd[it, pl.ds(c, 1), :] = jnp.sum(x, axis=0, keepdims=True)
-            msg_cd[it, pl.ds(ROWS + c, 1), :] = jnp.sum(x * sq[:, lanes(c)], axis=0, keepdims=True)
-            hi, lo = split_rows(x)
-            xh[0:FR, lanes(c)] = hi
-            xh[FR : 2 * FR, lanes(c)] = lo
-
         def inner_column(k, _):
-            back_column(k + 2, total_column(k + 2))
+            x = fwd[:, lanes(k + 2)] * total_column(k + 2)
+            sum_column(k + 2, x)
+            split_column(k + 2, x)
             return 0
 
         lax.fori_loop(0, 14, inner_column, 0, unroll=7)
+        group_send(msg_cd.at[it], got_cd.at[it], 10 + it)
+        cumulate(tri_up, loc2, 1, 8)
         to_low.wait_recv()
         to_up.wait_recv()
-        back_column(0, msg_b[2 * it, :, :FR] + has_lower * got_b[2 * it + 1, :, :FR])
-        back_column(1, msg_b[2 * it, :, FR:] + has_lower * got_b[2 * it + 1, :, FR:])
-        back_column(16, msg_b[2 * it + 1, :, :FR] + has_upper * got_b[2 * it, :, :FR])
-        back_column(17, msg_b[2 * it + 1, :, FR:] + has_upper * got_b[2 * it, :, FR:])
-        group_send(msg_cd.at[it], got_cd.at[it], 10 + it)
-        cumulate(tri_up, loc2)
+        for c, part, present in ((0, 2 * it + 1, has_lower), (16, 2 * it, has_upper)):
+            for half in range(2):
+                at = slice(half * FR, (half + 1) * FR)
+                mine = msg_b[2 * it if c == 0 else 2 * it + 1, :, at]
+                split_column(c + half, fwd[:, lanes(c + half)] * (mine + present * got_b[part, :, at]))
+        cumulate(tri_up, loc2, 0, 1)
+        cumulate(tri_up, loc2, 8, 9)
 
         def square_part(c, _):
             at = lanes(c, 256)
@@ -397,6 +441,11 @@
 
         lax.fori_loop(0, NCOL // 2, square_part, 0, unroll=9)
         group_wait(got_cd.at[it], 10 + it)
+        wide_wait(got_h.at[1 + it], 18 + 2 * it)
+        for k in range(NT):
+            for part, at in ((0, 0), (2, ROWS)):
+                got_cd[it, k, at : at + 2, :] += has_lower * got_h[1 + it, 0, k, part : part + 2, :]
+                got_cd[it, k, at + 16 : at + 18, :] += has_upper * got_h[1 + it, 1, k, part : part + 2, :]
         w = jnp.zeros((ROWS, FR), F32)
         mine = w
         carry = w
@@ -479,6 +528,8 @@
         copy.wait_send()
     group_sent(got_a0, 4)
     group_sent(got_a1, 5)
+    for k in range(1 + ITERS):
+        wide_sent(got_h.at[k], 16 + 2 * k)
     for it in range(ITERS):
         remote(msg_b.at[2 * it], got_b.at[2 * it], 6 + 2 * it, lower).wait_send()
         remote(msg_b.at[2 * it + 1], got_b.at[2 * it + 1], 7 + 2 * it, upper).wait_send()
@@ -507,9 +558,10 @@
         vm((2 * ROWS, FR), F32), vm((ROWS, FR), F32), vm((ITERS, 2 * ROWS, FR), F32),
         vm((NT, 2 * ROWS, FR), F32), vm((NT, ROWS, FR), F32), vm((ITERS, NT, 2 * ROWS, FR), F32),
         vm((2 * ITERS, FR, 2 * FR), F32), vm((2 * ITERS, FR, 2 * FR), F32),
+        vm((1 + ITERS, 2, 8, FR), F32), vm((1 + ITERS, 2, NT, 8, FR), F32),
         vm((2 * ITERS, 1, FR), F32),
         vm((ITERS, len(STAGES[0]), 1, FR), F32), vm((ITERS, len(STAGES[1]), 1, FR), F32),
-        pltpu.SemaphoreType.DMA((16,)), pltpu.SemaphoreType.DMA((16,)), pltpu.SemaphoreType.DMA((6,)),
+        pltpu.SemaphoreType.DMA((22,)), pltpu.SemaphoreType.DMA((22,)), pltpu.SemaphoreType.DMA((6,)),
     ]
     anywhere = pl.BlockSpec(memory_space=pl.ANY)
     in_vmem = pl.BlockSpec(memory_space=pltpu.VMEM)

time: 71.4 us -> 64.6 us (0.905)
  Pallas kernels: 68.7 us -> 61.9 us
    pallas_call x1, Pallas kernels: 68.7 us -> 61.9 us  [per_device(): pl.pallas_call(kernel, out_shape=(pltpu.VMEM((NEU, FR), F32), pltpu.VMEM(...]
where the time goes in v3:
time: 64.6 us; the launch traced here: 64.5 us
  Pallas kernels  61.9 us (96%)
  local copies, waits for them, and re-layouts  1.94 us (3%)
    pallas_call x1, Pallas kernels, per_device(): pl.pallas_call(kernel, out_shape=(pltpu.VMEM((NEU, FR), F32), pltpu.VMEM(...  61.9 us
    unnamed x2, local copies, waits for them, and re-layouts  1.94 us

profile of v3, /device:TPU:1, one launch (start us, length us, event | category | flops | bytes accessed | tf_op | source)
XLA Modules:
  0.0 64.5 jit_solution(337026005892002711)
XLA Ops:
  0.6 61.9 %deconvolve.1 = (f32[2048,128]{1,0:T(8,128)S(1)}, f32[2048,128]{1,0:T(8,128)S(1)}) custom-call(bf16[8192,128]{1,0:T(8,128)(2,1)} %rec_hbm.1, bf16[8192,256]{1,0:T(8,128)(2,1)} %foot_hbm.1, s32[4,32]{1,0:T(4,128)} %bitcast.4, f32[16,128]{1,0:T(8,128)} %bitcast.3, f32[1,128]{1,0:T(1,128)} %bitcast.5, f32[2048,128]{1,0:T(8,128)} %spk_hbm.1), custom_call_target="tpu_custom_call" | custom-call | tf_op jit(solution)/shard_map/deconvolve/pallas_call | solution.py:568
  62.6 1.0 %copy.10 = f32[2048,128]{1,0:T(8,128)} copy(f32[2048,128]{1,0:T(8,128)S(1)} %get-tuple-element.2) | data formatting | bytes 2097152
  63.6 1.0 %copy.11 = f32[2048,128]{1,0:T(8,128)} copy(f32[2048,128]{1,0:T(8,128)S(1)} %get-tuple-element.3) | data formatting | bytes 2097152

commit v4 on v3

--- a/solution.py
+++ b/solution.py
@@ -57,8 +57,8 @@
     out_spk, out_tr,
     foot_raw, rec_raw, spk_raw, decay, fgain, pat, fp, fpt, rec_t,
     cur, grad, fwd, inv, sq, xh, loc, loc2, acc_n, acc_s, val_n, val_s,
-    lgb, tri_lo, tri_up, decd, tab_u, tab_e, tab_t, tab_q, tab_c, row_w, row_c,
-    halo_spk, halo_dec, msg_a0, msg_a1, msg_cd, got_a0, got_a1, got_cd,
+    seam, lgb, tri_lo, tri_up, decd, tab_u, tab_e, tab_t, tab_q, tab_c, row_w, row_c,
+    halo_spk, halo_dec, msg_a0, msg_a1, msg_cda, msg_cdb, got_a0, got_a1, got_cda, got_cdb,
     msg_b, got_b, msg_h, got_h, msg_e, got_e0, got_e1,
     ss, rs, ls,
 ):
@@ -120,7 +120,8 @@
 
     msg_a0[...] = jnp.zeros_like(msg_a0)
     msg_a1[...] = jnp.zeros_like(msg_a1)
-    msg_cd[...] = jnp.zeros_like(msg_cd)
+    msg_cda[...] = jnp.zeros_like(msg_cda)
+    msg_cdb[...] = jnp.zeros_like(msg_cdb)
     msg_a0[ROWS + NCOL : ROWS + NCOL + 1, :] = jnp.broadcast_to(lg_tot, (1, FR))
     msg_a0[ROWS + NCOL + 1 : ROWS + NCOL + 2, :] = jnp.broadcast_to(lg_mid, (1, FR))
     decd[...] = jnp.ones_like(decd)
@@ -264,16 +265,16 @@
 
         lax.fori_loop(first, last, body, 0, unroll=last - first)
 
-    def put_columns(value):
-        def body(c, before):
-            y = value(c)
-            val_n[:, lanes(c)] = y.astype(BF16)
-            turned = pltpu.roll(y, NEU_BLOCK, 1)
-            val_s[:, lanes(c)] = jnp.where(low_half, before, turned).astype(BF16)
-            return turned
-
-        last = lax.fori_loop(0, NCOL, body, jnp.zeros((FR, FR), F32), unroll=6)
-        val_s[:, NCOL * FR : (NCOL + 1) * FR] = last.astype(BF16)
+    def put_column(c, y, before):
+        val_n[:, lanes(c)] = y.astype(BF16)
+        turned = pltpu.roll(y, NEU_BLOCK, 1)
+        val_s[:, lanes(c)] = jnp.where(low_half, before, turned).astype(BF16)
+        return turned
+
+    def put_moved(c, turned, after):
+        val_s[:, lanes(c + 1)] = jnp.where(low_half, turned, after).astype(BF16)
+
+    nothing = jnp.zeros((FR, FR), F32)
 
     low_row = lax.broadcasted_iota(jnp.int32, (1, FR), 1) < NEU_BLOCK
     m_lo = jnp.where(low_row, 1.0, 0.0).astype(BF16)
@@ -373,13 +374,23 @@
                 loc[:, lanes(c)] = y
             return y
 
-        put_columns(traces_of)
-
-        def edge_blocks(k, _):
-            residual_step(k + 12 * lax.div(k, 2))
+        def put_trace(c, before):
+            return put_column(c, traces_of(c), before)
+
+        def put_and_step(c, before):
+            turned = put_trace(c, before)
+            residual_step(c - 3)
+            return turned
+
+        def step_only(i, _):
+            residual_step(i)
             return 0
 
-        lax.fori_loop(0, 4, edge_blocks, 0, unroll=4)
+        seam[0] = lax.fori_loop(0, 5, put_trace, nothing, unroll=5)
+        lax.fori_loop(0, 2, step_only, 0, unroll=2)
+        seam[1] = put_trace(14, nothing)
+        put_moved(17, lax.fori_loop(15, NCOL, put_trace, seam[1], unroll=3), nothing)
+        lax.fori_loop(14, 16, step_only, 0, unroll=2)
         msg_b[2 * it, :, :FR] = total_column(0, first=True)
         msg_b[2 * it, :, FR:] = total_column(1)
         msg_b[2 * it + 1, :, :FR] = total_column(16)
@@ -389,9 +400,12 @@
         to_low.start()
         to_up.start()
 
-        def sum_column(c, x):
-            msg_cd[it, pl.ds(c, 1), :] = jnp.sum(x, axis=0, keepdims=True)
-            msg_cd[it, pl.ds(ROWS + c, 1), :] = jnp.sum(x * sq[:, lanes(c)], axis=0, keepdims=True)
+        parts_cd = ((msg_cda, got_cda, 0, 8, 10 + it), (msg_cdb, got_cdb, 8, 16, 22 + it))
+
+        def sum_column(c, x, part):
+            msg, _, base, n, _ = parts_cd[part]
+            msg[it, pl.ds(c - base, 1), :] = jnp.sum(x, axis=0, keepdims=True)
+            msg[it, pl.ds(n + c - base, 1), :] = jnp.sum(x * sq[:, lanes(c)], axis=0, keepdims=True)
 
         def split_column(c, x):
             hi, lo = split_rows(x)
@@ -399,27 +413,30 @@
             xh[FR : 2 * FR, lanes(c)] = lo
 
         for c, part, half in ((0, 2 * it, 0), (1, 2 * it, 1), (16, 2 * it + 1, 0), (17, 2 * it + 1, 1)):
-            sum_column(c, fwd[:, lanes(c)] * msg_b[part, :, half * FR : (half + 1) * FR])
+            sum_column(c, fwd[:, lanes(c)] * msg_b[part, :, half * FR : (half + 1) * FR], part - 2 * it)
         msg_h[1 + it] = jnp.zeros_like(msg_h[1 + it])
-        for side, c in ((0, 16), (1, 0)):
-            msg_h[1 + it, side, 0:2, :] = msg_cd[it, c : c + 2, :]
-            msg_h[1 + it, side, 2:4, :] = msg_cd[it, ROWS + c : ROWS + c + 2, :]
+        msg_h[1 + it, 0, 0:2, :] = msg_cdb[it, 8:10, :]
+        msg_h[1 + it, 0, 2:4, :] = msg_cdb[it, 24:26, :]
+        msg_h[1 + it, 1, 0:2, :] = msg_cda[it, 0:2, :]
+        msg_h[1 + it, 1, 2:4, :] = msg_cda[it, 8:10, :]
         wide_send(msg_h.at[1 + it], got_h.at[1 + it], 18 + 2 * it)
 
-        def inner_blocks(k, _):
-            residual_step(k + 2)
-            return 0
-
-        lax.fori_loop(0, 12, inner_blocks, 0, unroll=12)
-
-        def inner_column(k, _):
-            x = fwd[:, lanes(k + 2)] * total_column(k + 2)
-            sum_column(k + 2, x)
-            split_column(k + 2, x)
-            return 0
-
-        lax.fori_loop(0, 14, inner_column, 0, unroll=7)
-        group_send(msg_cd.at[it], got_cd.at[it], 10 + it)
+        def inner_columns(first, last, part):
+            def inner_column(c, _):
+                x = fwd[:, lanes(c)] * total_column(c)
+                sum_column(c, x, part)
+                split_column(c, x)
+                return 0
+
+            lax.fori_loop(first, last, inner_column, 0, unroll=last - first)
+            msg, got, _, _, k = parts_cd[part]
+            group_send(msg.at[it], got.at[it], k)
+
+        before = lax.fori_loop(5, 11, put_and_step, seam[0], unroll=6)
+        inner_columns(2, 8, 0)
+        put_moved(13, lax.fori_loop(11, 14, put_and_step, before, unroll=3), seam[1])
+        lax.fori_loop(11, 14, step_only, 0, unroll=3)
+        inner_columns(8, 16, 1)
         cumulate(tri_up, loc2, 1, 8)
         to_low.wait_recv()
         to_up.wait_recv()
@@ -440,28 +457,32 @@
             return 0
 
         lax.fori_loop(0, NCOL // 2, square_part, 0, unroll=9)
-        group_wait(got_cd.at[it], 10 + it)
+        def carries(part):
+            _, got, base, n, k = parts_cd[part]
+            group_wait(got.at[it], k)
+            at = part * 8
+            present = (has_lower, has_upper)[part]
+            for k in range(NT):
+                got[it, k, at : at + 2, :] += present * got_h[1 + it, part, k, 0:2, :]
+                got[it, k, n + at : n + at + 2, :] += present * got_h[1 + it, part, k, 2:4, :]
+            rows = slice(base, base + n)
+            w = jnp.zeros((n, FR), F32)
+            mine = w
+            carry = w
+            for j in range(NT - 1, -1, -1):
+                at = slot_of(j)
+                mine = jnp.where(tm == j, w, mine)
+                carry = carry + tab_c[j, rows, :] * (got[it, at, n : 2 * n, :] + tab_q[j, rows, :] * w)
+                w = tab_e[j, rows, :] * got[it, at, 0:n, :] + tab_t[j, rows, :] * w
+            row_w[rows, :] = tab_u[tm, rows, :] * mine
+            row_c[rows, :] = carry
+
         wide_wait(got_h.at[1 + it], 18 + 2 * it)
-        for k in range(NT):
-            for part, at in ((0, 0), (2, ROWS)):
-                got_cd[it, k, at : at + 2, :] += has_lower * got_h[1 + it, 0, k, part : part + 2, :]
-                got_cd[it, k, at + 16 : at + 18, :] += has_upper * got_h[1 + it, 1, k, part : part + 2, :]
-        w = jnp.zeros((ROWS, FR), F32)
-        mine = w
-        carry = w
-        for j in range(NT - 1, -1, -1):
-            at = slot_of(j)
-            mine = jnp.where(tm == j, w, mine)
-            carry = carry + tab_c[j] * (got_cd[it, at, ROWS : 2 * ROWS, :] + tab_q[j] * w)
-            w = tab_e[j] * got_cd[it, at, 0:ROWS, :] + tab_t[j] * w
-        row_w[...] = tab_u[tm] * mine
-        row_c[...] = carry
+        carries(0)
 
         def direction_of(c):
             at = lanes(c)
             return fwd[:, at] * (grad[:, at] + sq[:, at] * row_w[pl.ds(c, 1), :] + row_c[pl.ds(c, 1), :])
-
-        put_columns(direction_of)
 
         def gradient_column(c):
             at = lanes(c)
@@ -478,9 +499,21 @@
             g_sum = g_sum + jnp.sum((g * g).reshape(16, 8, FR), axis=0)
             return g_sum, p_sum
 
-        g_sum, p_sum = lax.fori_loop(
-            0, 16, image_step, (jnp.zeros((8, FR), F32), jnp.zeros((8, 2 * FR), F32)), unroll=16
-        )
+        def put_direction(c, before):
+            return put_column(c, direction_of(c), before)
+
+        def put_and_image(c, carried):
+            before, g_sum, p_sum = carried
+            turned = put_direction(c, before)
+            return (turned,) + image_step(c - 3, (g_sum, p_sum))
+
+        before = lax.fori_loop(0, 3, put_direction, nothing, unroll=3)
+        carried = (before, jnp.zeros((8, FR), F32), jnp.zeros((8, 2 * FR), F32))
+        carried = lax.fori_loop(3, 8, put_and_image, carried, unroll=5)
+        carries(1)
+        before, g_sum, p_sum = lax.fori_loop(8, NCOL, put_and_image, carried, unroll=10)
+        put_moved(17, before, nothing)
+        g_sum, p_sum = image_step(15, (g_sum, p_sum))
         g_row = jnp.sum(g_sum, axis=0, keepdims=True)
         p_row = jnp.sum(p_sum[:, :FR] + p_sum[:, FR:], axis=0, keepdims=True)
         total = jnp.where(
@@ -533,7 +566,8 @@
     for it in range(ITERS):
         remote(msg_b.at[2 * it], got_b.at[2 * it], 6 + 2 * it, lower).wait_send()
         remote(msg_b.at[2 * it + 1], got_b.at[2 * it + 1], 7 + 2 * it, upper).wait_send()
-        group_sent(got_cd.at[it], 10 + it)
+        group_sent(got_cda.at[it], 10 + it)
+        group_sent(got_cdb.at[it], 22 + it)
         for k, got_e in enumerate((got_e0, got_e1)):
             everything = got_e.at[it]
             remote(everything, everything, 12 + 2 * it + k, upper).wait_send()
@@ -549,19 +583,19 @@
         vm(wide, F32), vm(wide, F32), vm(wide, F32), vm(wide, F32), vm(wide, F32),
         vm((2 * FR, NCOL * FR), BF16), vm(wide, F32), vm(wide, F32), vm(wide, F32), vm(wide, F32),
         vm(wide, BF16), vm((FR, (NCOL + 1) * FR), BF16),
-        vm((FR, FR), F32), vm((FR, 2 * FR), BF16), vm((FR, 2 * FR), BF16),
+        vm((2, FR, FR), F32), vm((FR, FR), F32), vm((FR, 2 * FR), BF16), vm((FR, 2 * FR), BF16),
         vm((ROWS, FR), F32),
         vm((NT, ROWS, FR), F32), vm((NT, ROWS, FR), F32), vm((NT, ROWS, FR), F32),
         vm((NT, ROWS, FR), F32), vm((NT, ROWS, FR), F32),
         vm((ROWS, FR), F32), vm((ROWS, FR), F32),
         vm((2, FR, FR), F32), vm((2, 8, FR), F32),
-        vm((2 * ROWS, FR), F32), vm((ROWS, FR), F32), vm((ITERS, 2 * ROWS, FR), F32),
-        vm((NT, 2 * ROWS, FR), F32), vm((NT, ROWS, FR), F32), vm((ITERS, NT, 2 * ROWS, FR), F32),
+        vm((2 * ROWS, FR), F32), vm((ROWS, FR), F32), vm((ITERS, 16, FR), F32), vm((ITERS, 32, FR), F32),
+        vm((NT, 2 * ROWS, FR), F32), vm((NT, ROWS, FR), F32), vm((ITERS, NT, 16, FR), F32), vm((ITERS, NT, 32, FR), F32),
         vm((2 * ITERS, FR, 2 * FR), F32), vm((2 * ITERS, FR, 2 * FR), F32),
         vm((1 + ITERS, 2, 8, FR), F32), vm((1 + ITERS, 2, NT, 8, FR), F32),
         vm((2 * ITERS, 1, FR), F32),
         vm((ITERS, len(STAGES[0]), 1, FR), F32), vm((ITERS, len(STAGES[1]), 1, FR), F32),
-        pltpu.SemaphoreType.DMA((22,)), pltpu.SemaphoreType.DMA((22,)), pltpu.SemaphoreType.DMA((6,)),
+        pltpu.SemaphoreType.DMA((24,)), pltpu.SemaphoreType.DMA((24,)), pltpu.SemaphoreType.DMA((6,)),
     ]
     anywhere = pl.BlockSpec(memory_space=pl.ANY)
     in_vmem = pl.BlockSpec(memory_space=pltpu.VMEM)

time: 64.6 us -> 62.6 us (0.969)
  Pallas kernels: 61.9 us -> 59.9 us
    pallas_call x1, Pallas kernels: 61.9 us -> 59.9 us  [per_device(): pl.pallas_call(kernel, out_shape=(pltpu.VMEM((NEU, FR), F32), pltpu.VMEM(...]
where the time goes in v4:
time: 62.6 us; the launch traced here: 62.5 us
  Pallas kernels  59.9 us (96%)
  local copies, waits for them, and re-layouts  1.94 us (3%)
  between operations  0.64 us (1%)
    pallas_call x1, Pallas kernels, per_device(): pl.pallas_call(kernel, out_shape=(pltpu.VMEM((NEU, FR), F32), pltpu.VMEM(...  59.9 us
    unnamed x2, local copies, waits for them, and re-layouts  1.94 us

profile of v4, /device:TPU:1, one launch (start us, length us, event | category | flops | bytes accessed | tf_op | source)
XLA Modules:
  0.0 62.5 jit_solution(2133732854313040023)
XLA Ops:
  0.6 59.9 %deconvolve.1 = (f32[2048,128]{1,0:T(8,128)S(1)}, f32[2048,128]{1,0:T(8,128)S(1)}) custom-call(bf16[8192,128]{1,0:T(8,128)(2,1)} %rec_hbm.1, bf16[8192,256]{1,0:T(8,128)(2,1)} %foot_hbm.1, s32[4,32]{1,0:T(4,128)} %bitcast.4, f32[16,128]{1,0:T(8,128)} %bitcast.3, f32[1,128]{1,0:T(1,128)} %bitcast.5, f32[2048,128]{1,0:T(8,128)} %spk_hbm.1), custom_call_target="tpu_custom_call" | custom-call | tf_op jit(solution)/shard_map/deconvolve/pallas_call | solution.py:602
  60.6 1.0 %copy.10 = f32[2048,128]{1,0:T(8,128)} copy(f32[2048,128]{1,0:T(8,128)S(1)} %get-tuple-element.2) | data formatting | bytes 2097152
  61.6 1.0 %copy.11 = f32[2048,128]{1,0:T(8,128)} copy(f32[2048,128]{1,0:T(8,128)S(1)} %get-tuple-element.3) | data formatting | bytes 2097152

commit v5 on v4

--- a/solution.py
+++ b/solution.py
@@ -182,7 +182,7 @@
         return 0
 
 
-    lax.fori_loop(0, 16, arrange, 0, unroll=4)
+    lax.fori_loop(0, 4, arrange, 0, unroll=4)
 
     pl.semaphore_wait(barrier, len(group) + len(crossed))
 
@@ -238,7 +238,7 @@
     for copy in halo:
         copy.start()
 
-    lax.fori_loop(16, 32, arrange, 0, unroll=4)
+    lax.fori_loop(4, 32, arrange, 0, unroll=4)
 
     load_rec.wait()
 

time: 62.6 us -> 62.2 us (level)
  no operation moved by 1% of the time
where the time goes in v5:
time: 62.2 us; the launch traced here: 62.1 us
  Pallas kernels  59.6 us (96%)
  local copies, waits for them, and re-layouts  1.94 us (3%)
  between operations  0.64 us (1%)
    pallas_call x1, Pallas kernels, per_device(): pl.pallas_call(kernel, out_shape=(pltpu.VMEM((NEU, FR), F32), pltpu.VMEM(...  59.6 us
    unnamed x2, local copies, waits for them, and re-layouts  1.94 us

profile of v5, /device:TPU:1, one launch (start us, length us, event | category | flops | bytes accessed | tf_op | source)
XLA Modules:
  0.0 62.1 jit_solution(6991356561295983794)
XLA Ops:
  0.6 59.6 %deconvolve.1 = (f32[2048,128]{1,0:T(8,128)S(1)}, f32[2048,128]{1,0:T(8,128)S(1)}) custom-call(bf16[8192,128]{1,0:T(8,128)(2,1)} %rec_hbm.1, bf16[8192,256]{1,0:T(8,128)(2,1)} %foot_hbm.1, s32[4,32]{1,0:T(4,128)} %bitcast.4, f32[16,128]{1,0:T(8,128)} %bitcast.3, f32[1,128]{1,0:T(1,128)} %bitcast.5, f32[2048,128]{1,0:T(8,128)} %spk_hbm.1), custom_call_target="tpu_custom_call" | custom-call | tf_op jit(solution)/shard_map/deconvolve/pallas_call | solution.py:602
  60.2 1.0 %copy.10 = f32[2048,128]{1,0:T(8,128)} copy(f32[2048,128]{1,0:T(8,128)S(1)} %get-tuple-element.2) | data formatting | bytes 2097152
  61.2 1.0 %copy.11 = f32[2048,128]{1,0:T(8,128)} copy(f32[2048,128]{1,0:T(8,128)S(1)} %get-tuple-element.3) | data formatting | bytes 2097152
